TPU v7x, 32 devices: a whole 2x2x4 slice. The times are simulated.
32 devices in a mesh: dp: 16 (over z, x, core), group: 2 (over y).
Axes of the slice: x: 2, y: 2, z: 4, core: 2. Of those that a mesh axis runs over, the one named last changes fastest.
Arguments:
- queries: bfloat16 [4096, 256], P('dp'), may hold values from -110 to 110
- item_features: bfloat16 [4096, 2048], P('dp', 'group'), may hold values from -6 to 6
- corpus: bfloat16 [32768, 2048], P('dp', 'group'), may hold values from -6 to 6
- sample_ids: int32 [16384], P('dp'), may hold values from 0 to 2047
- sample_shift: bfloat16 [16384], P('dp'), may hold values from -2 to 2
- w1: bfloat16 [2048, 1024], P(None, 'group'), may hold values from -0.125 to 0.125
- w2: bfloat16 [1024, 256], P('group'), may hold values from -0.1875 to 0.1875
Outputs:
- query_loss: float32 [4096], P(('dp', 'group'))
- grad_query: float32 [4096, 256], P(('dp', 'group'))
- grad_w1: float32 [2048, 1024], P(None, 'group')
- grad_w2: float32 [1024, 256], P('group')
Inputs may be any that keep to these rules, and one draw needn't show every extreme that they name: sample_ids[k] is a row of the corpus block of the dp index that holds position k.
All inputs are finite; a program needn't handle non-finite values.
Results may differ from a plain program's by a relative error of at most 0.02.
The roundings to bfloat16 on the way count: a program that leaves them out, or rounds other values in their place, can miss the bound.
Values may be sent and summed in bfloat16 or wider, within the bound.
A program may use at most 128 MiB of HBM per device.

v0:
```python
import jax
import jax.numpy as jnp
from jax import lax
from jax.sharding import PartitionSpec as P


def alternate(head_part, tail_part, groups):
    emb_cols = head_part.shape[1]
    joined = jnp.concatenate(
        [head_part.reshape(groups, -1, emb_cols), tail_part.reshape(groups, -1, emb_cols)], 1
    )
    return joined.reshape(-1, emb_cols)


def per_device(queries, item_features, corpus, sample_ids, sample_shift, w1, w2):
    groups = lax.axis_size("group")
    member = lax.axis_index("group")
    query_rows, emb_width = queries.shape
    quota_rows = query_rows // groups
    neg_rows = sample_ids.shape[0] // groups
    score_scale = emb_width ** (-0.5)
    block_rows = 256
    steps_count = query_rows // block_rows
    picked = jnp.take(corpus, sample_ids, axis=0)
    features_local = alternate(item_features, picked, groups)
    gathered = lax.all_gather(features_local, "group", axis=1, tiled=True)
    pre_act = jnp.dot(gathered, w1, preferred_element_type=jnp.float32)
    hidden = jnp.maximum(pre_act, 0.0).astype(jnp.bfloat16)
    partial_embed = jnp.dot(hidden, w2, preferred_element_type=jnp.float32)
    embedded = lax.psum_scatter(partial_embed, "group", scatter_dimension=0, tiled=True)
    inverse = lax.rsqrt(jnp.mean(embedded * embedded, -1, keepdims=True) + 1e-06)
    normed = (embedded * inverse).astype(jnp.bfloat16)
    shift_own = lax.dynamic_slice_in_dim(sample_shift, member * neg_rows, neg_rows)
    bias_own = jnp.concatenate([jnp.zeros((quota_rows,), jnp.bfloat16), -shift_own])
    stashed, bias_all = (
        lax.all_gather(normed, "dp", axis=0, tiled=True),
        lax.all_gather(bias_own, "dp", axis=0, tiled=True),
    )
    bias_wide = bias_all.astype(jnp.float32)
    query_blocks = queries.reshape(steps_count, block_rows, emb_width)

    def score_block(query_blk):
        return (
            score_scale
            * jnp.einsum("qe,ce->qc", query_blk, stashed, preferred_element_type=jnp.float32)
            + bias_wide
        )

    def row_stats(query_blk):
        logits = score_block(query_blk)
        highest = jnp.max(logits, -1)
        return (highest, jnp.sum(jnp.exp(logits - highest[:, None]), -1))

    highest, row_sum = lax.map(row_stats, query_blocks)
    highest = highest.reshape(query_rows)
    row_sum = row_sum.reshape(query_rows)
    largest = lax.pmax(highest, "group")
    row_sum = lax.psum(row_sum * jnp.exp(highest - largest), "group")
    highest = largest
    log_total = highest + jnp.log(row_sum)
    query_own = lax.dynamic_slice_in_dim(queries, member * quota_rows, quota_rows)
    positive_own = normed[:quota_rows].astype(jnp.float32)
    positive = score_scale * jnp.sum(query_own.astype(jnp.float32) * positive_own, -1)
    query_loss = lax.dynamic_slice_in_dim(log_total, member * quota_rows, quota_rows) - positive
    total_blocks = log_total.reshape(steps_count, block_rows)

    def softmax_block(query_blk, total_blk):
        return jnp.exp(score_block(query_blk) - total_blk[:, None]).astype(jnp.bfloat16)

    def accumulate(grad_acc, inputs):
        query_blk, total_blk = inputs
        softmax = softmax_block(query_blk, total_blk)
        grad_acc = grad_acc + jnp.einsum(
            "qc,qe->ce", softmax, query_blk, preferred_element_type=jnp.float32
        )
        return (grad_acc, jnp.dot(softmax, stashed, preferred_element_type=jnp.float32))

    grad_acc, grad_blocks = lax.scan(
        accumulate, jnp.zeros(stashed.shape, jnp.float32), (query_blocks, total_blocks)
    )
    grad_hat = lax.psum_scatter(grad_acc, "dp", scatter_dimension=0, tiled=True)
    query_sum = lax.psum_scatter(
        grad_blocks.reshape(query_rows, emb_width), "group", scatter_dimension=0, tiled=True
    )
    grad_query = score_scale * (query_sum - positive_own)
    target = jnp.concatenate(
        [query_own.astype(jnp.float32), jnp.zeros((neg_rows, emb_width), jnp.float32)], 0
    )
    grad_normed = score_scale * (grad_hat - target)
    along = jnp.sum(grad_normed * embedded, -1, keepdims=True)
    grad_embed = inverse * grad_normed - inverse**3 * embedded * along / emb_width
    grad_back = lax.all_gather(grad_embed.astype(jnp.bfloat16), "group", axis=0, tiled=True)
    grad_pre = jnp.where(
        pre_act > 0, jnp.dot(grad_back, w2.T, preferred_element_type=jnp.float32), 0.0
    ).astype(jnp.bfloat16)
    grad_w2 = jnp.einsum("rh,re->he", hidden, grad_back, preferred_element_type=jnp.float32)
    grad_w1 = jnp.einsum("rf,rh->fh", gathered, grad_pre, preferred_element_type=jnp.float32)
    grad_w1, grad_w2 = lax.psum((grad_w1, grad_w2), "dp")
    return (query_loss, grad_query, grad_w1, grad_w2)


def solution(mesh):
    in_specs = (
        P("dp", None),
        P("dp", "group"),
        P("dp", "group"),
        P("dp"),
        P("dp"),
        P(None, "group"),
        P("group", None),
    )
    out_specs = (P(("dp", "group")), P(("dp", "group"), None), P(None, "group"), P("group", None))
    return jax.shard_map(
        per_device, mesh=mesh, in_specs=in_specs, out_specs=out_specs, check_vma=False
    )
```

profile of v0, /device:TPU:0, one launch (start us, length us, event | category | flops | bytes accessed | tf_op | source)
XLA Modules:
  0.0 489.6 jit_solution(1353273792064433591)
XLA Ops:
  7.2 0.0 copy-start
  7.2 0.0 all-gather.4.cloned.1.call-start
  7.2 0.8 fusion.9
  8.1 0.7 compare_and_fusion
  8.8 8.7 %gather_fusion = bf16[1024,1024]{1,0:T(8,128)(2,1)} fusion(bf16[2048,1024]{1,0:T(8,128)(2,1)} %param.9, s32[1024]{0:T(1024)S(1)} %fusion.9), kind=kCustom, calls=%fused_computation | custom fusion | bytes 4198400 | tf_op jit(solution)/shard_map/jit(_take)/gather | solution.py:24
  17.5 0.0 copy-start.4
  17.5 1.9 broadcast_select_fusion
  19.4 0.0 copy-done.4
  19.4 1.7 pad_maximum_fusion
  21.2 0.0 all-gather.4.cloned.1.call-update
  21.2 0.0 copy-start.6
  21.2 0.0 reduce-scatter.4.cloned.1.call-start
  21.2 71.4 %all-gather.4.cloned.1.call-done = bf16[1280,2048]{1,0:T(8,128)(2,1)} async-done(((bf16[1280,1024]{1,0:T(8,128)(2,1)}), bf16[1280,2048]{1,0:T(8,128)(2,1)}) %all-gather.4.cloned.1.call-update) | async-done | bytes 5242896 | tf_op jit(solution)/shard_map/all_gather | solution.py:26
  92.6 0.0 copy-done
  92.6 4.8 fusion.14
  97.4 0.0 copy-start.2
  97.4 1.5 copy-done.2
  98.9 0.0 copy-done.6
  98.9 0.0 copy-start.7
  98.9 0.0 copy-start.3
  98.9 1.6 fusion.6
  100.4 0.0 reduce-scatter.4.cloned.1.call-update
  100.5 0.0 all-gather.6.cloned.1.call-start
  100.5 23.3 %reduce-scatter.4.cloned.1.call-done = f32[640,256]{1,0:T(8,128)} async-done(((f32[1280,256]{1,0:T(8,128)}), f32[640,256]{1,0:T(8,128)}) %reduce-scatter.4.cloned.1.call-update) | async-done | bytes 655376 | tf_op jit(solution)/shard_map/reduce_scatter | solution.py:30
  123.8 1.3 multiply_reduce_fusion.1
  125.1 2.0 multiply_convert_fusion
  127.1 0.0 all-gather.6.cloned.1.call-update
  127.1 0.0 reduce-scatter.8.cloned.1.call-start
  127.1 0.0 copy-done.7
  127.2 0.1 dynamic-slice_negate_fusion
  127.2 21.6 %all-gather = bf16[16,1,640]{2,1,0:T(2,128)(2,1)S(1)} all-gather(bf16[1,1,640]{2,1,0:T(2,128)(2,1)S(1)} %reshape.68), channel_id=1, replica_groups=mesh['dp'=16,'group'=2] {'dp'}, dimensions={0}, use_global_device_ids=true | all-gather | bytes 21760 | tf_op jit(solution)/shard_map/all_gather | solution.py:37
  148.8 34.4 %all-gather.6.cloned.1.call-done = bf16[10240,256]{1,0:T(8,128)(2,1)} async-done(((bf16[640,256]{1,0:T(8,128)(2,1)}), bf16[10240,256]{1,0:T(8,128)(2,1)}) %all-gather.6.cloned.1.call-update) | async-done | bytes 5242896 | tf_op jit(solution)/shard_map/all_gather | solution.py:36
  183.3 0.0 copy-done.3
  183.3 6.6 %fusion.13 = (f32[256]{0:T(256)S(1)}, f32[10240,256]{1,0:T(8,128)}) fusion(f32[10240]{0:T(1024)S(1)} %bitcast.18, bf16[10240,256]{1,0:T(8,128)(2,1)} %all-gather.6.cloned.1.call-done, bf16[256,256]{1,0:T(8,128)(2,1)S(1)} %copy-done.3), kind=kOutput, calls=%fused_computation.38 | convolution fusion | flops 1350041344 | bytes 15901696 | tf_op jit(solution)/shard_map/while/body/eval_jaxpr/qe,ce->qc/dot_general | solution.py:45
  189.9 4.9 %pmax.7 = f32[256]{0:T(256)S(1)} all-reduce(f32[256]{0:T(256)S(1)} %get-tuple-element.43), channel_id=1, replica_groups=mesh['dp'=16,'group'=2] {'group'}, use_global_device_ids=true, to_apply=%region_3.4 | all-reduce | flops 256 | bytes 2048 | tf_op jit(solution)/shard_map/pmax | solution.py:57
  194.8 5.2 %exponential_reduce_fusion = f32[256]{0:T(256)S(1)} fusion(f32[10240,256]{1,0:T(8,128)} %get-tuple-element.44, f32[256]{0:T(256)S(1)} %get-tuple-element.43), kind=kLoop, calls=%fused_computation.4 | loop fusion | flops 5242624 | bytes 10487808 | tf_op jit(solution)/shard_map/while/body/eval_jaxpr/reduce_sum | solution.py:52
  200.0 4.9 %psum.21 = f32[256]{0:T(256)S(1)} all-reduce(f32[256]{0:T(256)S(1)} %exponential_multiply_fusion), channel_id=1, replica_groups=mesh['dp'=16,'group'=2] {'group'}, use_global_device_ids=true, to_apply=%region_5.6 | all-reduce | flops 256 | bytes 2048 | tf_op jit(solution)/shard_map/psum | solution.py:58
  205.0 9.5 %fusion.3 = f32[10240,256]{1,0:T(8,128)} fusion(bf16[256,256]{1,0:T(8,128)(2,1)S(1)} %copy-done.3, f32[10240,256]{1,0:T(8,128)} %get-tuple-element.44, f32[256]{0:T(256)S(1)} %log_add_fusion), kind=kOutput, calls=%fused_computation.11 | convolution fusion | flops 1347420160 | bytes 21103616 | tf_op jit(solution)/shard_map/while/body/eval_jaxpr/qc,qe->ce/dot_general | solution.py:73
  214.5 0.0 reduce-scatter.8.cloned.1.call-update
  214.5 0.0 reduce-scatter.6.cloned.1.call-start
  214.6 0.0 copy-start.1
  214.6 8.4 %fusion.2 = f32[256,256]{1,0:T(8,128)} fusion(bf16[10240,256]{1,0:T(8,128)(2,1)} %all-gather.6.cloned.1.call-done, f32[10240,256]{1,0:T(8,128)} %get-tuple-element.44, f32[256]{0:T(256)S(1)} %log_add_fusion), kind=kOutput, calls=%fused_computation.10 | convolution fusion | flops 1347420160 | bytes 15991808 | tf_op jit(solution)/shard_map/while/body/eval_jaxpr/dot_general | solution.py:76
  223.0 0.0 reduce-scatter.6.cloned.1.call-update
  223.0 0.0 all-reduce.5.cloned.1.call-start
  223.1 109.3 %reduce-scatter.8.cloned.1.call-done = f32[640,256]{1,0:T(8,128)} async-done(((f32[10240,256]{1,0:T(8,128)}), f32[640,256]{1,0:T(8,128)}) %reduce-scatter.8.cloned.1.call-update) | async-done | bytes 655376 | tf_op jit(solution)/shard_map/reduce_scatter | solution.py:81
  332.3 0.0 copy-done.1
  332.3 1.3 multiply_reduce_fusion
  333.6 1.4 subtract_convert_fusion
  335.0 13.0 %all_gather.15 = bf16[1280,256]{1,0:T(8,128)(2,1)S(1)} all-gather(bf16[640,256]{1,0:T(8,128)(2,1)S(1)} %subtract_convert_fusion), channel_id=1, replica_groups=mesh['dp'=16,'group'=2] {'group'}, dimensions={0}, use_global_device_ids=true | all-gather | bytes 983040 | tf_op jit(solution)/shard_map/all_gather | solution.py:92
  348.0 8.6 %fusion.4 = f32[2048,512]{1,0:T(8,128)} fusion(bf16[1280,2048]{1,0:T(8,128)(2,1)} %all-gather.4.cloned.1.call-done, bf16[1280,256]{1,0:T(8,128)(2,1)S(1)} %all_gather.15, bf16[512,256]{1,0:T(8,128)(2,1)S(1)} %copy-done.6, f32[1280,512]{1,0:T(8,128)} %copy-done.2), kind=kOutput, calls=%fused_computation.12 | convolution fusion | flops 3021864960 | bytes 12976128 | tf_op jit(solution)/shard_map/rf,rh->fh/dot_general | solution.py:97
  356.7 3.1 fusion.5
  359.7 0.0 all-reduce.5.cloned.1.call-update
  359.8 0.0 reduce-scatter.6.cloned.1.call-done
  359.8 1.6 fusion.8
  361.4 0.6 multiply_subtract_fusion
  362.0 115.3 %all-reduce.5.cloned.1.call-done = (f32[2048,512]{1,0:T(8,128)}, f32[512,256]{1,0:T(8,128)}) async-done(((f32[2048,512]{1,0:T(8,128)}, f32[512,256]{1,0:T(8,128)}), (f32[2048,512]{1,0:T(8,128)}, f32[512,256]{1,0:T(8,128)})) %all-reduce.5.cloned.1.call-update) | async-done | bytes 4718608 | tf_op jit(solution)/shard_map/psum | solution.py:98
  477.2 0.0 copy-start.5
  477.2 4.7 copy.13
  481.9 0.0 copy-done.5
  481.9 0.8 copy.14
  (8 shorter events, 0.1 us)
Async XLA Ops:
  7.2 85.4 %copy-start = (bf16[2048,512]{1,0:T(8,128)(2,1)S(1)}, bf16[2048,512]{1,0:T(8,128)(2,1)}, u32[]{:S(2)}) copy-start(bf16[2048,512]{1,0:T(8,128)(2,1)} %param.12) | copy-start | bytes 6291460
  7.2 85.4 %all-gather.4.cloned.1.call-start = ((), (), s32[]{:S(2)}) async-start(), calls=%async_computation.3 | async-start | bytes 7864320 | tf_op jit(solution)/shard_map/all_gather | solution.py:26
  17.5 1.9 copy-start.4
  21.2 77.7 %copy-start.6 = (bf16[512,256]{1,0:T(8,128)(2,1)S(1)}, bf16[512,256]{1,0:T(8,128)(2,1)}, u32[]{:S(2)}) copy-start(bf16[512,256]{1,0:T(8,128)(2,1)} %param.13) | copy-start | bytes 786436
  21.2 102.6 %reduce-scatter.4.cloned.1.call-start = ((), (), s32[]{:S(2)}) async-start(), calls=%async_computation.4 | async-start | bytes 1966080 | tf_op jit(solution)/shard_map/reduce_scatter | solution.py:30
  97.4 1.5 copy-start.2
  98.9 28.3 %copy-start.7 = (bf16[1024]{0:T(1024)(128)(2,1)S(1)}, bf16[1024]{0:T(1024)(128)(2,1)}, u32[]{:S(2)}) copy-start(bf16[1024]{0:T(1024)(128)(2,1)} %param.11) | copy-start | bytes 6148
  98.9 84.4 %copy-start.3 = (bf16[256,256]{1,0:T(8,128)(2,1)S(1)}, bf16[256,256]{1,0:T(8,128)(2,1)}, u32[]{:S(2)}) copy-start(bf16[256,256]{1,0:T(8,128)(2,1)} %param.7) | copy-start | bytes 393220
  100.5 82.8 %all-gather.6.cloned.1.call-start = ((), (), s32[]{:S(2)}) async-start(), calls=%async_computation.5 | async-start | bytes 5570560 | tf_op jit(solution)/shard_map/all_gather | solution.py:36
  127.1 205.3 %reduce-scatter.8.cloned.1.call-start = ((), (), s32[]{:S(2)}) async-start(), calls=%async_computation.7 | async-start | bytes 11141120 | tf_op jit(solution)/shard_map/reduce_scatter | solution.py:81
  214.5 145.3 %reduce-scatter.6.cloned.1.call-start = ((), (), s32[]{:S(2)}) async-start(), calls=%async_computation.6 | async-start | bytes 393216 | tf_op jit(solution)/shard_map/reduce_scatter | solution.py:82
  214.6 117.7 %copy-start.1 = (f32[640,256]{1,0:T(8,128)S(1)}, f32[640,256]{1,0:T(8,128)}, u32[]{:S(2)}) copy-start(f32[640,256]{1,0:T(8,128)} %reduce-scatter.4.cloned.1.call-done) | copy-start | bytes 1966084
  223.0 254.2 %all-reduce.5.cloned.1.call-start = ((), (), s32[]{:S(2)}) async-start(), calls=%async_computation.8 | async-start | bytes 9437184 | tf_op jit(solution)/shard_map/psum | solution.py:98
  477.2 4.7 copy-start.5
Sparse Core Ops, SparseCore 0:
  21.3 71.2 all-gather.3
  100.6 23.1 reduce-scatter.3
  127.2 56.0 all-gather.5
  214.6 117.6 reduce-scatter.7
  334.5 13.7 reduce-scatter.5
  359.9 117.3 all-reduce.4
where the time goes:
time: 490 us
  waiting for transfers between devices  354 us (72%)
  blocking collectives  44.4 us (9%)
  matrix products  42.6 us (9%)
  other arithmetic  18.6 us (4%)
  local copies, waits for them, and re-layouts  15.8 us (3%)
  between operations  14.2 us (3%)
    psum x1, waiting for transfers between devices, per_device(): grad_w1, grad_w2 = lax.psum((grad_w1, grad_w2), 'dp')  115 us
    reduce_scatter x1, waiting for transfers between devices, per_device(): grad_hat = lax.psum_scatter(grad_acc, 'dp', scatter_dimension=0, tiled=True)  109 us
    all_gather x1, waiting for transfers between devices, per_device(): gathered = lax.all_gather(features_local, 'group', axis=1, tiled=True)  71.4 us
    all_gather x1, waiting for transfers between devices, per_device(): lax.all_gather(normed, 'dp', axis=0, tiled=True)  34.4 us
    reduce_scatter x1, waiting for transfers between devices, per_device(): lax.psum_scatter(partial_embed, 'group', scatter_dimension=0, tiled=True)  23.3 us
    all_gather x1, blocking collectives, per_device(): lax.all_gather(bias_own, 'dp', axis=0, tiled=True)  21.6 us
    all_gather x1, blocking collectives, per_device(): lax.all_gather(grad_embed.astype(jnp.bfloat16), 'group', axis=0, tiled=True)  13 us
  transfers between devices with their start and end apart: 6, of which 5 were waited for; matrix products, arithmetic and copies ran while one was open for 5% of the time, Pallas kernels for 0%

commit v1 on v0

v1 whole, which is shorter than its diff:
```python
import jax
import jax.numpy as jnp
from jax import lax
from jax.sharding import PartitionSpec as P

F32 = jnp.float32
BF16 = jnp.bfloat16
LANES = 128


def mm(a, b):
    return jnp.dot(a, b, preferred_element_type=F32)


def pack(x):
    return jnp.concatenate([x[:, i : i + LANES] for i in range(0, x.shape[1], LANES)], 0)


def unpack(x, rows, cols):
    x = x.reshape(x.shape[0], cols // LANES, rows, LANES)
    return jnp.concatenate([x[:, i].reshape(-1, LANES) for i in range(cols // LANES)], 1)


def per_device(queries, item_features, corpus, sample_ids, sample_shift, w1, w2):
    groups = lax.axis_size("group")
    member = lax.axis_index("group")
    n_dp = lax.axis_size("dp")
    d = lax.axis_index("dp")
    query_rows, emb = queries.shape
    quota = query_rows // groups
    negs = sample_ids.shape[0] // groups
    rows = quota + negs
    fg = item_features.shape[1]
    scale = emb ** (-0.5)

    def shift(x, s):
        return lax.ppermute(x, "group", [(i, (i + s) % groups) for i in range(groups)])

    def at(x, i):
        return lax.dynamic_index_in_dim(x, lax.rem(i, groups), 0, keepdims=False)

    w1_rows, w2_rows = w1.shape[0] // n_dp, w2.shape[0] // n_dp
    w1_piece = pack(lax.dynamic_slice_in_dim(w1, d * w1_rows, w1_rows))
    w2_piece = pack(lax.dynamic_slice_in_dim(w2, d * w2_rows, w2_rows))
    piece = jnp.concatenate([w1_piece, w2_piece], 0)
    pieces = [pack(queries)] + [shift(piece, s) for s in range(1, groups)]
    shared = lax.all_gather(jnp.concatenate(pieces, 0), "dp", axis=0, tiled=False)
    nq, n1, n2 = pieces[0].shape[0], w1_piece.shape[0], w2_piece.shape[0]
    q_all = unpack(shared[:, :nq], query_rows, emb)
    w1s, w2s = [w1], [w2]
    for s in range(1, groups):
        at0 = nq + (s - 1) * (n1 + n2)
        w1s.append(unpack(shared[:, at0 : at0 + n1], w1_rows, w1.shape[1]))
        w2s.append(unpack(shared[:, at0 + n1 : at0 + n1 + n2], w2_rows, emb))

    picked = corpus.at[sample_ids].get(mode="promise_in_bounds")
    local = jnp.concatenate(
        [item_features.reshape(groups, quota, fg), picked.reshape(groups, negs, fg)], 1
    )
    mine = [at(local, member)] + [shift(at(local, member + s), s) for s in range(1, groups)]
    feats = jnp.zeros((rows, groups * fg), BF16)
    for s in range(groups):
        feats = lax.dynamic_update_slice_in_dim(
            feats, mine[s], lax.rem(member + groups - s, groups) * fg, 1
        )
    local, feats = lax.optimization_barrier((local, feats))
    rest_rows = (groups - 1) * rows
    rest = jnp.zeros((rest_rows, groups * fg), BF16)
    for s in range(groups):
        blocks = jnp.concatenate([at(local, member + s + t) for t in range(1, groups)], 0)
        if s > 0:
            blocks = shift(blocks, s)
        rest = lax.dynamic_update_slice_in_dim(
            rest, blocks, lax.rem(member + groups - s, groups) * fg, 1
        )

    embedded = jnp.zeros((rows, emb), F32)
    pre_own = None
    for s in range(groups):
        pre = mm(feats, w1s[s])
        hid = jnp.maximum(pre, 0.0).astype(BF16)
        if s == 0:
            pre_own, hid_own = pre, hid
        embedded = embedded + mm(hid, w2s[s])
    inverse = lax.rsqrt(jnp.mean(embedded * embedded, -1, keepdims=True) + 1e-06)
    normed = (embedded * inverse).astype(BF16)
    shift_own = lax.dynamic_slice_in_dim(sample_shift, member * negs, negs).astype(F32)
    bias = jnp.concatenate([jnp.zeros((quota,), F32), -shift_own])

    logits = scale * lax.dot_general(
        q_all, normed, (((1,), (1,)), ((), ())), preferred_element_type=F32
    ) + bias
    axes = ("dp", "group")
    top = jnp.max(logits, -1)
    row_sum = jnp.sum(jnp.exp(logits - top[:, None]), -1)
    largest = lax.pmax(top, axes)
    row_sum = lax.psum(row_sum * jnp.exp(top - largest), axes)
    log_total = largest + jnp.log(row_sum)
    softmax = jnp.exp(logits - log_total[:, None]).astype(BF16)

    query_own = lax.dynamic_slice_in_dim(queries, member * quota, quota).astype(F32)
    positive_own = normed[:quota].astype(F32)
    positive = scale * jnp.sum(query_own * positive_own, -1)
    query_loss = (
        lax.dynamic_slice_in_dim(log_total, d * query_rows + member * quota, quota) - positive
    )
    grad_hat = lax.dot_general(
        softmax, q_all, (((0,), (0,)), ((), ())), preferred_element_type=F32
    )
    query_part = mm(softmax, normed)
    query_sum = lax.psum_scatter(query_part, axes, scatter_dimension=0, tiled=True)
    grad_query = scale * (query_sum - positive_own)

    target = jnp.concatenate([query_own, jnp.zeros((negs, emb), F32)], 0)
    grad_normed = scale * (grad_hat - target)
    along = jnp.sum(grad_normed * embedded, -1, keepdims=True)
    grad_embed = (
        inverse * grad_normed - inverse**3 * embedded * along / emb
    ).astype(BF16)

    pre_rest = mm(rest, w1)
    hid_rest = jnp.maximum(pre_rest, 0.0).astype(BF16)
    back = jnp.concatenate(
        [grad_embed] + [shift(grad_embed, (groups - t) % groups) for t in range(1, groups)], 0
    )
    mask = jnp.concatenate([pre_own, pre_rest], 0) > 0
    grad_pre = jnp.where(mask, mm(back, w2.T), 0.0).astype(BF16)
    hid_all = jnp.concatenate([hid_own, hid_rest], 0)
    over_rows = (((0,), (0,)), ((), ()))
    grad_w2 = lax.dot_general(hid_all, back, over_rows, preferred_element_type=F32)
    feats_all = jnp.concatenate([feats, rest], 0)
    grad_w1 = lax.dot_general(feats_all, grad_pre, over_rows, preferred_element_type=F32)
    grad_w1, grad_w2 = lax.psum((grad_w1, grad_w2), "dp")
    return (query_loss, grad_query, grad_w1, grad_w2)


def solution(mesh):
    in_specs = (
        P("dp", None),
        P("dp", "group"),
        P("dp", "group"),
        P("dp"),
        P("dp"),
        P(None, "group"),
        P("group", None),
    )
    out_specs = (P(("dp", "group")), P(("dp", "group"), None), P(None, "group"), P("group", None))
    return jax.shard_map(
        per_device, mesh=mesh, in_specs=in_specs, out_specs=out_specs, check_vma=False
    )
```

time: 490 us -> 471 us (0.961)
  waiting for transfers between devices: 354 us -> 280 us
  blocking collectives: 44.4 us -> 79.6 us
  local copies, waits for them, and re-layouts: 15.8 us -> 36.8 us
  matrix products: 42.6 us -> 31.8 us
  starting transfers between devices: 0.25 us -> 9.36 us
    all_gather x2 -> x1, waiting for transfers between devices: 106 us -> 8.23 us  [per_device(): lax.all_gather(jnp.concatenate(pieces, 0), 'dp', axis=0, tiled=False)]
    ppermute x0 -> x4, waiting for transfers between devices: none -> 93 us  [shift(): lax.ppermute(x, 'group', [(i, (i + s) % groups) for i in range(groups)])]
    reduce_scatter x3 -> x1, waiting for transfers between devices: 133 us -> 61.2 us  [per_device(): lax.psum_scatter(query_part, axes, scatter_dimension=0, tiled=True)]
    psum x1, blocking collectives: 4.94 us -> 40.3 us  [per_device(): row_sum = lax.psum(row_sum * jnp.exp(top - largest), axes)]
    all_gather x2 -> x0, blocking collectives: 34.6 us -> none  [the longest x1 21.6 us: per_device(): lax.all_gather(bias_own, 'dp', axis=0, tiled=True)]
    pmax x1, blocking collectives: 4.92 us -> 39.3 us  [per_device(): largest = lax.pmax(top, axes)]
    dot_general x7 -> x9, matrix products: 42.6 us -> 31.8 us  [the longest x5 13.5 us: mm(): return jnp.dot(a, b, preferred_element_type=F32)]
    ppermute x0 -> x4, starting transfers between devices: none -> 9.24 us  [shift(): lax.ppermute(x, 'group', [(i, (i + s) % groups) for i in range(groups)])]
  transfers between devices with their start and end apart: 6 -> 7, of which waited for: 5 -> 7; matrix products, arithmetic and copies ran while one was open for 5% -> 9% of each run, Pallas kernels for 0% -> 0%
where the time goes in v1:
time: 471 us; the launch traced here: 470 us
  waiting for transfers between devices  280 us (59%)
  blocking collectives  79.6 us (17%)
  local copies, waits for them, and re-layouts  36.8 us (8%)
  matrix products  31.8 us (7%)
  other arithmetic  18.9 us (4%)
  between operations  14.1 us (3%)
  starting transfers between devices  9.36 us (2%)
    psum x1, waiting for transfers between devices, per_device(): grad_w1, grad_w2 = lax.psum((grad_w1, grad_w2), 'dp')  117 us
    ppermute x4, waiting for transfers between devices, shift(): lax.ppermute(x, 'group', [(i, (i + s) % groups) for i in range(groups)])  93 us
    reduce_scatter x1, waiting for transfers between devices, per_device(): lax.psum_scatter(query_part, axes, scatter_dimension=0, tiled=True)  61.2 us
    psum x1, blocking collectives, per_device(): row_sum = lax.psum(row_sum * jnp.exp(top - largest), axes)  40.3 us
    pmax x1, blocking collectives, per_device(): largest = lax.pmax(top, axes)  39.3 us
    unnamed x49, local copies, waits for them, and re-layouts  15.5 us
    dot_general x5, matrix products, mm(): return jnp.dot(a, b, preferred_element_type=F32)  13.5 us
  transfers between devices with their start and end apart: 7, of which 7 were waited for; matrix products, arithmetic and copies ran while one was open for 9% of the time, Pallas kernels for 0%

profile of v1, /device:TPU:0, one launch (start us, length us, event | category | flops | bytes accessed | tf_op | source)
XLA Modules:
  0.0 470.5 jit_solution(16945653480433188150)
XLA Ops:
  7.2 0.0 all-gather.3.cloned.1.call-start
  7.2 0.8 dynamic-slice_dynamic-update-slice_fusion.3
  8.0 0.8 dynamic-slice_dynamic-update-slice_fusion.2
  8.7 0.8 dynamic-slice_dynamic-update-slice_fusion.1
  9.5 0.8 dynamic-slice_dynamic-update-slice_fusion
  10.3 0.7 constant_dynamic-update-slice_fusion.1
  11.0 0.7 constant_dynamic-update-slice_fusion
  11.7 3.0 collective-permute-start
  14.7 0.9 fusion.55
  15.5 3.0 collective-permute-done
  18.5 0.7 pad_maximum_fusion.10
  19.2 0.0 all-gather.3.cloned.1.call-update
  19.3 0.0 reduce-scatter.2.cloned.1.call-start
  19.3 0.7 fusion.40
  20.0 7.8 %gather_fusion = bf16[1024,1024]{1,0:T(8,128)(2,1)S(1)} fusion(bf16[2048,1024]{1,0:T(8,128)(2,1)} %param.9, s32[1024]{0:T(1024)S(1)} %fusion.40), kind=kCustom, calls=%fused_computation | custom fusion | bytes 4198400 | tf_op jit(solution)/shard_map/gather | solution.py:56
  27.8 1.2 fusion.26
  29.0 1.7 collective-permute-start.1
  30.7 0.1 convert_negate_fusion
  30.8 0.3 broadcast.39.clone
  31.1 0.2 fusion.24
  31.3 1.7 pad_maximum_fusion
  33.0 26.2 %collective-permute-done.1 = bf16[640,1024]{1,0:T(8,128)(2,1)} collective-permute-done((bf16[640,1024]{1,0:T(8,128)(2,1)}, bf16[640,1024]{1,0:T(8,128)(2,1)}, u32[]{:S(2)}, u32[]{:S(2)}) %collective-permute-start.1) | collective-permute-done | bytes 1310752 | tf_op jit(solution)/shard_map/ppermute | solution.py:37
  59.2 1.5 constant_dynamic-update-slice_fusion.3
  60.8 2.6 maximum_convert_fusion.1
  63.4 0.8 copy-done.9
  64.2 0.4 fusion.58
  64.6 8.2 %all-gather.3.cloned.1.call-done = bf16[17408,128]{1,0:T(8,128)(2,1)} async-done(((bf16[1088,128]{1,0:T(8,128)(2,1)}), bf16[17408,128]{1,0:T(8,128)(2,1)}) %all-gather.3.cloned.1.call-update) | async-done | bytes 4456464 | tf_op jit(solution)/shard_map/all_gather | solution.py:47
  72.8 2.6 fusion.51
  75.4 1.0 slice.90
  76.4 1.4 fusion.53
  77.8 0.7 fusion.54
  78.4 4.1 multiply_reduce_fusion.1
  82.6 0.1 fusion.52
  82.8 4.8 %fusion = (f32[4096]{0:T(1024)S(1)}, f32[4096,640]{0,1:T(8,128)}) fusion(f32[640]{0:T(1024)S(1)} %concatenate.42, bf16[640,256]{0,1:T(8,128)(2,1)S(1)} %multiply_convert_fusion, bf16[4096,128]{1,0:T(8,128)(2,1)S(1)} %bitcast.51, bf16[4096,128]{1,0:T(8,128)(2,1)S(1)} %bitcast.49), kind=kOutput, calls=%fused_computation.4 | convolution fusion | flops 1354231808 | bytes 12929536 | tf_op jit(solution)/shard_map/dot_general | solution.py:90
  87.7 39.3 %pmax.7 = f32[4096]{0:T(1024)S(1)} all-reduce(f32[4096]{0:T(1024)S(1)} %get-tuple-element.35), channel_id=1, replica_groups=mesh['dp'=16,'group'=2] {'dp','group'}, use_global_device_ids=true, to_apply=%region_2.3 | all-reduce | flops 4096 | bytes 32768 | tf_op jit(solution)/shard_map/pmax | solution.py:96
  126.9 6.4 %exponential_reduce_fusion = f32[4096]{0:T(1024)S(1)} fusion(f32[4096,640]{0,1:T(8,128)} %get-tuple-element.36, f32[4096]{0:T(1024)S(1)} %get-tuple-element.35, f32[640]{0:T(1024)S(1)} %concatenate.42), kind=kLoop, calls=%fused_computation.2 | loop fusion | flops 10481664 | bytes 10521088 | tf_op jit(solution)/shard_map/reduce_sum | solution.py:95
  133.3 40.3 %psum.21 = f32[4096]{0:T(1024)S(1)} all-reduce(f32[4096]{0:T(1024)S(1)} %exponential_multiply_fusion), channel_id=1, replica_groups=mesh['dp'=16,'group'=2] {'dp','group'}, use_global_device_ids=true, to_apply=%region_4.5 | all-reduce | flops 4096 | bytes 32768 | tf_op jit(solution)/shard_map/psum | solution.py:97
  173.6 6.3 %exponential_convert_fusion = bf16[4096,640]{0,1:T(8,128)(2,1)S(1)} fusion(f32[4096,640]{0,1:T(8,128)} %get-tuple-element.36, f32[4096]{0:T(1024)S(1)} %log_add_fusion, f32[640]{0:T(1024)S(1)} %concatenate.42), kind=kLoop, calls=%fused_computation.1 | loop fusion | flops 10485760 | bytes 15747584 | tf_op jit(solution)/shard_map/convert_element_type | solution.py:99
  179.9 2.3 copy-done
  182.2 3.8 fusion.59
  186.1 0.0 all-reduce.5.cloned.1.call-start
  186.2 2.6 dynamic-slice_bitcast_fusion
  188.8 2.3 collective-permute-start.2
  191.1 0.1 copy.17
  191.2 0.3 broadcast.39
  191.5 1.4 copy-done.1
  193.0 0.2 bitcast_dynamic-update-slice_fusion
  193.1 53.1 %collective-permute-done.2 = bf16[640,1024]{1,0:T(8,128)(2,1)} collective-permute-done((bf16[640,1024]{1,0:T(8,128)(2,1)}, bf16[640,1024]{1,0:T(8,128)(2,1)}, u32[]{:S(2)}, u32[]{:S(2)}) %collective-permute-start.2) | collective-permute-done | bytes 1310752 | tf_op jit(solution)/shard_map/ppermute | solution.py:37
  246.2 1.5 constant_dynamic-update-slice_fusion.2
  247.7 4.0 multiply_reduce_fusion
  251.8 0.1 subtract_convert_fusion
  251.9 2.2 collective-permute-start.3
  254.1 2.6 maximum_convert_fusion
  256.7 10.7 %collective-permute-done.3 = bf16[640,256]{0,1:T(8,128)(2,1)S(1)} collective-permute-done((bf16[640,256]{0,1:T(8,128)(2,1)S(1)}, bf16[640,256]{0,1:T(8,128)(2,1)S(1)}, u32[]{:S(2)}, u32[]{:S(2)}) %collective-permute-start.3) | collective-permute-done | bytes 327712 | tf_op jit(solution)/shard_map/ppermute | solution.py:37
  267.4 1.4 fusion.27
  268.8 0.7 copy-done.4
  269.5 8.0 %fusion.1 = f32[2048,512]{1,0:T(8,128)} fusion(bf16[640,2048]{1,0:T(8,128)(2,1)S(1)} %copy-done.4, bf16[640,2048]{1,0:T(8,128)(2,1)} %copy-done.5, bf16[512,256]{1,0:T(8,128)(2,1)} %param.13, f32[640,512]{1,0:T(8,128)} %get-tuple-element.40, f32[640,512]{1,0:T(8,128)} %get-tuple-element.32, bf16[640,256]{0,1:T(8,128)(2,1)} %copy-done.17, ...), kind=kOutput, calls=%fused_computation.5 | convolution fusion | flops 3034316800 | bytes 12976128 | tf_op jit(solution)/shard_map/dot_general | solution.py:132
  277.5 61.2 %reduce-scatter.2.cloned.1.call-done = f32[128,256]{0,1:T(8,128)} async-done(((f32[4096,256]{0,1:T(8,128)}), f32[128,256]{0,1:T(8,128)}) %reduce-scatter.2.cloned.1.call-update) | async-done | bytes 131088 | tf_op jit(solution)/shard_map/reduce_scatter | solution.py:111
  338.7 1.0 fusion.39
  339.7 0.8 copy.14
  340.4 0.6 multiply_subtract_fusion
  341.0 117.5 %all-reduce.5.cloned.1.call-done = (f32[2048,512]{1,0:T(8,128)}, f32[512,256]{1,0:T(8,128)}) async-done(((f32[2048,512]{1,0:T(8,128)}, f32[512,256]{1,0:T(8,128)}), (f32[2048,512]{1,0:T(8,128)}, f32[512,256]{1,0:T(8,128)})) %all-reduce.5.cloned.1.call-update) | async-done | bytes 4718608 | tf_op jit(solution)/shard_map/psum | solution.py:133
  458.5 4.7 copy.29
  463.2 0.8 copy.30
  (46 shorter events, 0.2 us)
Async XLA Ops:
  7.2 65.7 %all-gather.3.cloned.1.call-start = ((), (), s32[]{:S(2)}) async-start(), calls=%async_computation.2 | async-start | bytes 4734976 | tf_op jit(solution)/shard_map/all_gather | solution.py:47
  11.7 6.8 %collective-permute-start = (bf16[576,128]{1,0:T(8,128)(2,1)S(1)}, bf16[576,128]{1,0:T(8,128)(2,1)S(1)}, u32[]{:S(2)}, u32[]{:S(2)}) collective-permute-start(bf16[576,128]{1,0:T(8,128)(2,1)S(1)} %constant_dynamic-update-slice_fusion), channel_id=1, source_target_pairs={{0,1},{1,0},{2,3},{3,2},{4,5},{5,4},{6,7},{7,6},{8,9},{9,8},{10,11... | collective-permute-start | bytes 442376 | tf_op jit(solution)/shard_map/ppermute | solution.py:37
  19.3 319.4 %reduce-scatter.2.cloned.1.call-start = ((), (), s32[]{:S(2)}) async-start(), calls=%async_computation.1 | async-start | bytes 4325376 | tf_op jit(solution)/shard_map/reduce_scatter | solution.py:111
  20.0 7.8 %copy-start.2 = (bf16[256,1024]{1,0:T(8,128)(2,1)S(1)}, bf16[256,1024]{1,0:T(8,128)(2,1)}, u32[]{:S(2)}) copy-start(bf16[256,1024]{1,0:T(8,128)(2,1)} %param.8) | copy-start | bytes 1572868
  27.8 2.9 copy-start.16
  29.0 30.3 %collective-permute-start.1 = (bf16[640,1024]{1,0:T(8,128)(2,1)}, bf16[640,1024]{1,0:T(8,128)(2,1)}, u32[]{:S(2)}, u32[]{:S(2)}) collective-permute-start(bf16[640,1024]{1,0:T(8,128)(2,1)} %fusion.26), channel_id=1, source_target_pairs={{0,1},{1,0},{2,3},{3,2},{4,5},{5,4},{6,7},{7,6},{8,9},{9,8},{10,11... | collective-permute-start | bytes 3932168 | tf_op jit(solution)/shard_map/ppermute | solution.py:37
  33.0 27.7 %copy-start.14 = (bf16[2048,512]{1,0:T(8,128)(2,1)S(1)}, bf16[2048,512]{1,0:T(8,128)(2,1)}, u32[]{:S(2)}) copy-start(bf16[2048,512]{1,0:T(8,128)(2,1)} %param.12) | copy-start | bytes 6291460
  60.7 2.6 copy-start.5
  60.7 3.4 copy-start.12
  63.4 0.8 copy-start.9
  82.7 4.9 %copy-start.6 = (bf16[16,1,256,128]{3,2,1,0:T(8,128)(2,1)}, bf16[16,1,256,128]{3,2,1,0:T(8,128)(2,1)S(1)}, u32[]{:S(2)}) copy-start(bf16[16,1,256,128]{3,2,1,0:T(8,128)(2,1)S(1)} %get-tuple-element.16) | copy-start | bytes 3145732
  82.8 4.9 %copy-start.8 = (bf16[16,1,256,128]{3,2,1,0:T(8,128)(2,1)}, bf16[16,1,256,128]{3,2,1,0:T(8,128)(2,1)S(1)}, u32[]{:S(2)}) copy-start(bf16[16,1,256,128]{3,2,1,0:T(8,128)(2,1)S(1)} %get-tuple-element.17) | copy-start | bytes 3145732
  179.9 2.3 copy-start
  186.1 5.0 %copy-start.13 = (bf16[256,256]{1,0:T(8,128)(2,1)S(1)}, bf16[256,256]{1,0:T(8,128)(2,1)}, u32[]{:S(2)}) copy-start(bf16[256,256]{1,0:T(8,128)(2,1)} %param.7) | copy-start | bytes 393220
  186.1 272.4 %all-reduce.5.cloned.1.call-start = ((), (), s32[]{:S(2)}) async-start(), calls=%async_computation.3 | async-start | bytes 9437184 | tf_op jit(solution)/shard_map/psum | solution.py:133
  186.1 61.5 %slice-start = ((s8[5242880]{0:T(1024)(128)(4,1)}), s8[1048576]{0:T(1024)(128)(4,1)S(1)}, s32[]{:S(2)}) async-start(s8[5242880]{0:T(1024)(128)(4,1)} %bitcast.39), calls=%async_computation.4 | async-start | bytes 2097152
  188.8 57.4 %collective-permute-start.2 = (bf16[640,1024]{1,0:T(8,128)(2,1)}, bf16[640,1024]{1,0:T(8,128)(2,1)}, u32[]{:S(2)}, u32[]{:S(2)}) collective-permute-start(bf16[640,1024]{1,0:T(8,128)(2,1)} %dynamic-slice_bitcast_fusion), channel_id=1, source_target_pairs={{0,1},{1,0},{2,3},{3,2},{4,5},{5,4},{6,7},{7,6},{8,9},{9,8},{10,11... | collective-permute-start | bytes 3932168 | tf_op jit(solution)/shard_map/ppermute | solution.py:37
  191.2 1.8 copy-start.1
  191.2 56.4 %slice-start.1 = ((s8[5242880]{0:T(1024)(128)(4,1)}), s8[4194304]{0:T(1024)(128)(4,1)S(1)}, s32[]{:S(2)}) async-start(s8[5242880]{0:T(1024)(128)(4,1)} %bitcast.39), calls=%async_computation.5 | async-start | bytes 8388608
  193.0 54.7 %copy-start.7 = (bf16[16,1,256,128]{3,2,1,0:T(8,128)(2,1)S(1)}, bf16[16,1,256,128]{3,2,1,0:T(8,128)(2,1)}, u32[]{:S(2)}) copy-start(bf16[16,1,256,128]{3,2,1,0:T(8,128)(2,1)} %copy-done.6) | copy-start | bytes 3145732
  247.7 6.4 %copy-start.3 = (bf16[640,2048]{1,0:T(8,128)(2,1)}, bf16[640,2048]{1,0:T(8,128)(2,1)S(1)}, u32[]{:S(2)}) copy-start(bf16[640,2048]{1,0:T(8,128)(2,1)S(1)} %constant_dynamic-update-slice_fusion.2) | copy-start | bytes 7864324
  247.7 6.4 %copy-start.15 = (bf16[2048,512]{1,0:T(8,128)(2,1)S(1)}, bf16[2048,512]{1,0:T(8,128)(2,1)}, u32[]{:S(2)}) copy-start(bf16[2048,512]{1,0:T(8,128)(2,1)} %param.12) | copy-start | bytes 6291460
  251.9 15.5 %copy-start.10 = (bf16[640,512]{1,0:T(8,128)(2,1)S(1)}, bf16[640,512]{1,0:T(8,128)(2,1)}, u32[]{:S(2)}) copy-start(bf16[640,512]{1,0:T(8,128)(2,1)} %copy-done.9) | copy-start | bytes 1966084
  251.9 15.5 %collective-permute-start.3 = (bf16[640,256]{0,1:T(8,128)(2,1)S(1)}, bf16[640,256]{0,1:T(8,128)(2,1)S(1)}, u32[]{:S(2)}, u32[]{:S(2)}) collective-permute-start(bf16[640,256]{0,1:T(8,128)(2,1)S(1)} %subtract_convert_fusion), channel_id=1, source_target_pairs={{0,1},{1,0},{2,3},{3,2},{4,5},{5,4},{6,7},{7,6},{8,9},{9,8},{10,11... | collective-permute-start | bytes 983048 | tf_op jit(solution)/shard_map/ppermute | solution.py:37
  267.4 1.4 copy-start.17
  267.4 2.1 copy-start.4
  458.5 4.7 copy-start.11
Sparse Core Ops, SparseCore 0:
  19.4 53.4 all-gather.2
  186.2 152.4 reduce-scatter.1
  343.0 115.4 all-reduce.4

commit v2 on v1

--- a/solution.py
+++ b/solution.py
@@ -1,11 +1,253 @@
+import functools
+
 import jax
 import jax.numpy as jnp
 from jax import lax
+from jax.experimental import pallas as pl
+from jax.experimental.pallas import tpu as pltpu
 from jax.sharding import PartitionSpec as P
 
 F32 = jnp.float32
 BF16 = jnp.bfloat16
 LANES = 128
+MESH = pl.DeviceIdType.MESH
+ANY = pl.BlockSpec(memory_space=pl.ANY)
+VMEM = pl.BlockSpec(memory_space=pltpu.VMEM)
+
+
+def bits_of(n):
+    return [1 << i for i in range(n.bit_length() - 1)]
+
+
+def partner(axis, step):
+    i = lax.axis_index(axis)
+    bit = lax.rem(lax.div(i, step), 2)
+    return bit, {axis: i + step - 2 * step * bit}
+
+
+def greet(peers):
+    barrier = pltpu.get_barrier_semaphore()
+    for peer in peers:
+        pl.semaphore_signal(barrier, inc=1, device_id=peer, device_id_type=MESH)
+    pl.semaphore_wait(barrier, len(peers))
+
+
+def score_kernel(groups, n_dp, local, queries, normed, normed_t, bias,
+                 total_ref, hat_ref, part_ref, rest_ref,
+                 logits, stats, arrived, send_sem, recv_sem, fsend, frecv):
+    tiles, cols, width = logits.shape
+    emb = normed.shape[1]
+    scale = emb ** (-0.5)
+    member = lax.axis_index("group")
+    rounds = [("dp", b) for b in bits_of(n_dp)] + [("group", b) for b in bits_of(groups)]
+    peers = [partner(a, b)[1] for a, b in rounds]
+    others = [lax.rem(member + s, groups) for s in range(1, groups)]
+    extra = [{"group": o} for o in others] if groups > 2 else []
+    greet(peers + extra)
+    copies = []
+    for s in range(1, groups):
+        for t in range(1, groups):
+            k = (s - 1) * (groups - 1) + t - 1
+            copy = pltpu.make_async_remote_copy(
+                src_ref=local.at[lax.rem(member + s + t, groups)],
+                dst_ref=rest_ref.at[s - 1, t - 1],
+                send_sem=fsend.at[k], recv_sem=frecv.at[k],
+                device_id={"group": others[s - 1]}, device_id_type=MESH)
+            copy.start()
+            copies.append(copy)
+
+    def first(i, carry):
+        q = queries[pl.ds(pl.multiple_of(i * width, width), width), :]
+        block = scale * lax.dot_general(
+            normed[...], q, (((1,), (1,)), ((), ())), preferred_element_type=F32) + bias[...]
+        logits[i] = block
+        top = jnp.max(block, 0, keepdims=True)
+        stats[0, 0, pl.ds(i, 1), :] = top
+        stats[0, 1, pl.ds(i, 1), :] = jnp.sum(jnp.exp(block - top), 0, keepdims=True)
+        return carry
+
+    lax.fori_loop(0, tiles, first, 0)
+    for r, peer in enumerate(peers):
+        copy = pltpu.make_async_remote_copy(
+            src_ref=stats.at[r], dst_ref=arrived.at[r],
+            send_sem=send_sem.at[r], recv_sem=recv_sem.at[r],
+            device_id=peer, device_id_type=MESH)
+        copy.start()
+        copy.wait()
+        m0, s0, m1, s1 = stats[r, 0], stats[r, 1], arrived[r, 0], arrived[r, 1]
+        top = jnp.maximum(m0, m1)
+        stats[r + 1, 0] = top
+        stats[r + 1, 1] = s0 * jnp.exp(m0 - top) + s1 * jnp.exp(m1 - top)
+    last = len(peers)
+    total_ref[...] = stats[last, 0] + jnp.log(stats[last, 1])
+    hat_ref[...] = jnp.zeros_like(hat_ref)
+
+    def second(i, carry):
+        at_i = pl.ds(pl.multiple_of(i * width, width), width)
+        p = jnp.exp(logits[i] - total_ref[pl.ds(i, 1), :]).astype(BF16)
+        hat_ref[...] += mm(p, queries[at_i, :])
+        part_ref[at_i, :] = mm(normed_t[...], p).T
+        return carry
+
+    lax.fori_loop(0, tiles, second, 0)
+    for copy in copies:
+        copy.wait()
+
+
+def score(groups, n_dp, local, queries, normed, bias):
+    rows, fg = local.shape[1:]
+    width = 256
+    total, emb = queries.shape
+    tiles = total // width
+    rounds = len(bits_of(n_dp)) + len(bits_of(groups))
+    n_copies = (groups - 1) ** 2
+    return pl.pallas_call(
+        functools.partial(score_kernel, groups, n_dp),
+        out_shape=(
+            jax.ShapeDtypeStruct((tiles, width), F32),
+            jax.ShapeDtypeStruct((rows, emb), F32),
+            jax.ShapeDtypeStruct((total, emb), F32),
+            jax.ShapeDtypeStruct((groups - 1, groups - 1, rows, fg), BF16),
+        ),
+        in_specs=[ANY, VMEM, VMEM, VMEM, VMEM],
+        out_specs=(VMEM, VMEM, VMEM, ANY),
+        scratch_shapes=[
+            pltpu.VMEM((tiles, rows, width), F32),
+            pltpu.VMEM((rounds + 1, 2, tiles, width), F32),
+            pltpu.VMEM((rounds, 2, tiles, width), F32),
+            pltpu.SemaphoreType.DMA((rounds,)),
+            pltpu.SemaphoreType.DMA((rounds,)),
+            pltpu.SemaphoreType.DMA((n_copies,)),
+            pltpu.SemaphoreType.DMA((n_copies,)),
+        ],
+        compiler_params=pltpu.CompilerParams(
+            collective_id=0, has_side_effects=True, vmem_limit_bytes=44 << 20),
+        name="score",
+    )(local, queries, normed, normed.T, bias)
+
+
+def reduce_kernel(plans, n_peers_of, *refs):
+    n = len(plans)
+    ins, outs = refs[:n], refs[n : 2 * n]
+    accs, sends, recvs = (refs[2 * n + i * n : 3 * n + i * n] for i in range(3))
+    send_sem, recv_sem, gsend, grecv = refs[5 * n :]
+    greet([partner(a, b)[1] for a, b in n_peers_of])
+    live = {}
+
+    def begin(i, r):
+        rounds, bases, _ = plans[i]
+        bit, peer = partner(*rounds[r])
+        half = ins[i].shape[0] >> (r + 1)
+        at0 = ins[i].shape[0] - 2 * half
+
+        def stage(j, carry):
+            if r == 0:
+                block = ins[i][bases(j) + (1 - bit) * bases(half)]
+            else:
+                block = accs[i][(1 - bit) * half + j]
+            sends[i][at0 + j] = block.astype(BF16)
+            return carry
+
+        lax.fori_loop(0, half, stage, 0)
+        copy = pltpu.make_async_remote_copy(
+            src_ref=sends[i].at[pl.ds(at0, half)], dst_ref=recvs[i].at[pl.ds(at0, half)],
+            send_sem=send_sem.at[i, r], recv_sem=recv_sem.at[i, r],
+            device_id=peer, device_id_type=MESH)
+        copy.start()
+        live[i] = copy
+
+    def finish(i, r):
+        rounds, bases, _ = plans[i]
+        bit, _ = partner(*rounds[r])
+        half = ins[i].shape[0] >> (r + 1)
+        at0 = ins[i].shape[0] - 2 * half
+        live[i].wait()
+
+        def add(j, carry):
+            if r == 0:
+                block = ins[i][bases(j) + bit * bases(half)]
+            else:
+                block = accs[i][bit * half + j]
+            accs[i][j] = block + recvs[i][at0 + j].astype(F32)
+            return carry
+
+        lax.fori_loop(0, half, add, 0)
+
+    def place(i, r):
+        rounds = plans[i][0]
+        return sum(partner(*rounds[k])[0] * (ins[i].shape[0] >> (k + 1)) for k in range(r + 1))
+
+    def share(i, r):
+        peer = partner(*plans[i][0][r])[1]
+        span = pl.ds(place(i, r), ins[i].shape[0] >> (r + 1))
+        copy = pltpu.make_async_remote_copy(
+            src_ref=outs[i].at[span], dst_ref=outs[i].at[span],
+            send_sem=gsend.at[i, r], recv_sem=grecv.at[i, r],
+            device_id=peer, device_id_type=MESH)
+        copy.start()
+        live[i] = copy
+
+    def advance(i, step):
+        rounds, _, gather = plans[i]
+        k = len(rounds)
+        if 0 < step <= k:
+            finish(i, step - 1)
+        if step < k:
+            begin(i, step)
+        elif step == k and not gather:
+            outs[i][0] = accs[i][0]
+        elif gather and step <= 2 * k:
+            if step == k:
+                outs[i][place(i, k - 1)] = accs[i][0].astype(BF16)
+            else:
+                live[i].wait()
+            if step < 2 * k:
+                share(i, 2 * k - 1 - step)
+
+    steps = max(len(p[0]) * (2 if p[2] else 1) for p in plans) + 1
+    for step in range(steps):
+        for i in range(n):
+            advance(i, step)
+
+
+def bit_place(steps, j):
+    k = len(steps)
+    out = 0
+    for i, step in enumerate(steps):
+        weight = 1 << (k - 1 - i)
+        if isinstance(j, int):
+            out += (j // weight) % 2 * step
+        else:
+            out = out + lax.rem(lax.div(j, weight), 2) * step
+    return out
+
+
+def reduce_all(groups, n_dp, arrays):
+    plans = []
+    for x, rounds, gather in arrays:
+        n = x.shape[0]
+        if gather:
+            steps = [n >> (k + 1) for k in range(len(rounds))]
+        else:
+            steps = [b * groups if a == "dp" else b for a, b in rounds]
+        plans.append((rounds, functools.partial(bit_place, steps), gather))
+    xs = [x for x, _, _ in arrays]
+    most = max(len(p[0]) for p in plans)
+    peers = [("dp", b) for b in bits_of(n_dp)] + [("group", b) for b in bits_of(groups)]
+    sems = pltpu.SemaphoreType.DMA((len(xs), most))
+    return pl.pallas_call(
+        functools.partial(reduce_kernel, plans, peers),
+        out_shape=tuple(
+            jax.ShapeDtypeStruct(x.shape, BF16) if g else jax.ShapeDtypeStruct((1,) + x.shape[1:], F32)
+            for x, _, g in arrays),
+        in_specs=[VMEM] * len(xs),
+        out_specs=(VMEM,) * len(xs),
+        scratch_shapes=[pltpu.VMEM((x.shape[0] // 2,) + x.shape[1:], F32) for x in xs]
+        + [pltpu.VMEM(x.shape, BF16) for x in xs] * 2 + [sems] * 4,
+        compiler_params=pltpu.CompilerParams(
+            collective_id=1, has_side_effects=True, vmem_limit_bytes=48 << 20),
+        name="reduce_all",
+    )(*xs)
 
 
 def mm(a, b):
@@ -63,17 +305,6 @@
         feats = lax.dynamic_update_slice_in_dim(
             feats, mine[s], lax.rem(member + groups - s, groups) * fg, 1
         )
-    local, feats = lax.optimization_barrier((local, feats))
-    rest_rows = (groups - 1) * rows
-    rest = jnp.zeros((rest_rows, groups * fg), BF16)
-    for s in range(groups):
-        blocks = jnp.concatenate([at(local, member + s + t) for t in range(1, groups)], 0)
-        if s > 0:
-            blocks = shift(blocks, s)
-        rest = lax.dynamic_update_slice_in_dim(
-            rest, blocks, lax.rem(member + groups - s, groups) * fg, 1
-        )
-
     embedded = jnp.zeros((rows, emb), F32)
     pre_own = None
     for s in range(groups):
@@ -87,16 +318,18 @@
     shift_own = lax.dynamic_slice_in_dim(sample_shift, member * negs, negs).astype(F32)
     bias = jnp.concatenate([jnp.zeros((quota,), F32), -shift_own])
 
-    logits = scale * lax.dot_general(
-        q_all, normed, (((1,), (1,)), ((), ())), preferred_element_type=F32
-    ) + bias
-    axes = ("dp", "group")
-    top = jnp.max(logits, -1)
-    row_sum = jnp.sum(jnp.exp(logits - top[:, None]), -1)
-    largest = lax.pmax(top, axes)
-    row_sum = lax.psum(row_sum * jnp.exp(top - largest), axes)
-    log_total = largest + jnp.log(row_sum)
-    softmax = jnp.exp(logits - log_total[:, None]).astype(BF16)
+    log_total, grad_hat, query_part, landed = score(
+        groups, n_dp, local, q_all, normed, bias[:, None])
+    log_total = log_total.reshape(-1)
+    rest = jnp.zeros(((groups - 1) * rows, groups * fg), BF16)
+    for s in range(groups):
+        if s > 0:
+            blocks = landed[s - 1].reshape(-1, fg)
+        else:
+            blocks = jnp.concatenate([at(local, member + t) for t in range(1, groups)], 0)
+        rest = lax.dynamic_update_slice_in_dim(
+            rest, blocks, lax.rem(member + groups - s, groups) * fg, 1
+        )
 
     query_own = lax.dynamic_slice_in_dim(queries, member * quota, quota).astype(F32)
     positive_own = normed[:quota].astype(F32)
@@ -104,13 +337,6 @@
     query_loss = (
         lax.dynamic_slice_in_dim(log_total, d * query_rows + member * quota, quota) - positive
     )
-    grad_hat = lax.dot_general(
-        softmax, q_all, (((0,), (0,)), ((), ())), preferred_element_type=F32
-    )
-    query_part = mm(softmax, normed)
-    query_sum = lax.psum_scatter(query_part, axes, scatter_dimension=0, tiled=True)
-    grad_query = scale * (query_sum - positive_own)
-
     target = jnp.concatenate([query_own, jnp.zeros((negs, emb), F32)], 0)
     grad_normed = scale * (grad_hat - target)
     along = jnp.sum(grad_normed * embedded, -1, keepdims=True)
@@ -130,7 +356,27 @@
     grad_w2 = lax.dot_general(hid_all, back, over_rows, preferred_element_type=F32)
     feats_all = jnp.concatenate([feats, rest], 0)
     grad_w1 = lax.dot_general(feats_all, grad_pre, over_rows, preferred_element_type=F32)
-    grad_w1, grad_w2 = lax.psum((grad_w1, grad_w2), "dp")
+    dp_bits = bits_of(n_dp)
+    near, far = dp_bits[:1], dp_bits[:1:-1]
+    along_first = [("dp", b) for b in near + dp_bits[1:2] + far]
+    along_last = [("dp", b) for b in near + far + dp_bits[1:2]]
+    query_order = (
+        [("dp", near[0])]
+        + [("group", b) for b in bits_of(groups)]
+        + [("dp", b) for b in dp_bits[1:2] + far]
+    )
+    pad = -grad_w2.shape[0] % (16 * n_dp)
+    padded = jnp.pad(grad_w2, ((0, pad), (0, 0)))
+    halves = grad_w1.reshape(2, n_dp, -1, grad_w1.shape[1])
+    out_a, out_b, out_w2, query_sum = reduce_all(groups, n_dp, [
+        (halves[0], along_last, True),
+        (halves[1], along_first, True),
+        (padded.reshape(n_dp, -1, emb), along_first, True),
+        (query_part.reshape(n_dp * groups, quota, emb), query_order, False),
+    ])
+    grad_query = scale * (query_sum[0] - positive_own)
+    grad_w1 = jnp.concatenate([out_a, out_b], 0).reshape(grad_w1.shape).astype(F32)
+    grad_w2 = out_w2.reshape(padded.shape)[: grad_w2.shape[0]].astype(F32)
     return (query_loss, grad_query, grad_w1, grad_w2)
 
 

time: 471 us -> 234 us (0.50)
  waiting for transfers between devices: 280 us -> 36.5 us
  Pallas kernels: 0 us -> 104 us
  blocking collectives: 79.6 us -> 0 us
  matrix products: 31.8 us -> 22.3 us
    psum x1 -> x0, waiting for transfers between devices: 117 us -> none  [per_device(): grad_w1, grad_w2 = lax.psum((grad_w1, grad_w2), 'dp')]
    pallas_call x0 -> x2, Pallas kernels: none -> 104 us  [the longest x1 61.2 us: reduce_all(): pl.pallas_call(functools.partial(reduce_kernel, plans, peers), out_shape=...]
    ppermute x4 -> x3, waiting for transfers between devices: 93 us -> 30.7 us  [shift(): lax.ppermute(x, 'group', [(i, (i + s) % groups) for i in range(groups)])]
    reduce_scatter x1 -> x0, waiting for transfers between devices: 61.2 us -> none  [per_device(): lax.psum_scatter(query_part, axes, scatter_dimension=0, tiled=True)]
    psum x1 -> x0, blocking collectives: 40.3 us -> none  [per_device(): row_sum = lax.psum(row_sum * jnp.exp(top - largest), axes)]
    pmax x1 -> x0, blocking collectives: 39.3 us -> none  [per_device(): largest = lax.pmax(top, axes)]
    unnamed x49 -> x42, local copies, waits for them, and re-layouts: 15.5 us -> 4.58 us
    dot_general x2 -> x0, matrix products: 8.88 us -> none  [the longest x1 4.83 us: per_device(): lax.dot_general(q_all, normed, (((1,), (1,)), ((), ())), preferred_elemen...]
  transfers between devices with their start and end apart: 7 -> 4, of which waited for: 7 -> 4; matrix products, arithmetic and copies ran while one was open for 9% -> 12% of each run, Pallas kernels for 0% -> 0%
where the time goes in v2:
time: 234 us
  Pallas kernels  104 us (44%)
  waiting for transfers between devices  36.5 us (16%)
  local copies, waits for them, and re-layouts  34.5 us (15%)
  matrix products  22.3 us (10%)
  other arithmetic  16.6 us (7%)
  between operations  14.3 us (6%)
  starting transfers between devices  5.35 us (2%)
    pallas_call x1, Pallas kernels, reduce_all(): pl.pallas_call(functools.partial(reduce_kernel, plans, peers), out_shape=...  61.2 us
    pallas_call x1, Pallas kernels, score(): pl.pallas_call(functools.partial(score_kernel, groups, n_dp), out_shape=(...  42.9 us
    ppermute x3, waiting for transfers between devices, shift(): lax.ppermute(x, 'group', [(i, (i + s) % groups) for i in range(groups)])  30.7 us
    dot_general x4, matrix products, mm(): return jnp.dot(a, b, preferred_element_type=F32)  13.8 us
    dot_general x1, matrix products, per_device(): lax.dot_general(feats_all, grad_pre, over_rows, preferred_element_type=F32)  8 us
    gather x1, local copies, waits for them, and re-layouts, per_device(): picked = corpus.at[sample_ids].get(mode='promise_in_bounds')  7.7 us
    all_gather x1, waiting for transfers between devices, per_device(): lax.all_gather(jnp.concatenate(pieces, 0), 'dp', axis=0, tiled=False)  5.78 us
    ppermute x3, starting transfers between devices, shift(): lax.ppermute(x, 'group', [(i, (i + s) % groups) for i in range(groups)])  5.31 us
  transfers between devices with their start and end apart: 4, of which 4 were waited for; matrix products, arithmetic and copies ran while one was open for 12% of the time, Pallas kernels for 0%

profile of v2, /device:TPU:0, one launch (start us, length us, event | category | flops | bytes accessed | tf_op | source)
XLA Modules:
  0.0 233.5 jit_solution(11153009839632808861)
XLA Ops:
  7.2 0.0 all-gather.3.cloned.1.call-start
  7.2 0.8 dynamic-slice_dynamic-update-slice_fusion.3
  8.0 0.8 dynamic-slice_dynamic-update-slice_fusion.2
  8.7 0.8 dynamic-slice_dynamic-update-slice_fusion.1
  9.5 0.8 dynamic-slice_dynamic-update-slice_fusion
  10.3 0.7 constant_dynamic-update-slice_fusion.1
  11.0 0.7 constant_dynamic-update-slice_fusion
  11.7 3.0 %collective-permute-start = (bf16[576,128]{1,0:T(8,128)(2,1)S(1)}, bf16[576,128]{1,0:T(8,128)(2,1)S(1)}, u32[]{:S(2)}, u32[]{:S(2)}) collective-permute-start(bf16[576,128]{1,0:T(8,128)(2,1)S(1)} %constant_dynamic-update-slice_fusion), channel_id=1, source_target_pairs={{0,1},{1,0},{2,3},{3,2},{4,5},{5,4},{6,7},{7,6},{8,9},{9,8},{10,11... | collective-permute-start | bytes 442376 | tf_op jit(solution)/shard_map/ppermute | solution.py:279
  14.7 0.9 fusion.53
  15.5 3.0 %collective-permute-done = bf16[576,128]{1,0:T(8,128)(2,1)S(1)} collective-permute-done((bf16[576,128]{1,0:T(8,128)(2,1)S(1)}, bf16[576,128]{1,0:T(8,128)(2,1)S(1)}, u32[]{:S(2)}, u32[]{:S(2)}) %collective-permute-start) | collective-permute-done | bytes 147488 | tf_op jit(solution)/shard_map/ppermute | solution.py:279
  18.5 0.7 pad_maximum_fusion.7
  19.2 0.0 all-gather.3.cloned.1.call-update
  19.3 0.7 fusion.38
  20.0 7.7 %gather_fusion = bf16[1024,1024]{1,0:T(8,128)(2,1)S(1)} fusion(bf16[2048,1024]{1,0:T(8,128)(2,1)} %param.9, s32[1024]{0:T(1024)S(1)} %fusion.38), kind=kCustom, calls=%fused_computation | custom fusion | bytes 4198400 | tf_op jit(solution)/shard_map/gather | solution.py:298
  27.7 0.0 copy-start.1
  27.7 0.0 copy-start.3
  27.7 1.8 broadcast.37.clone
  29.6 1.9 constant_dynamic-update-slice_fusion.2
  31.5 1.7 collective-permute-start.1
  33.2 0.0 copy-done.14
  33.2 0.1 convert_negate_fusion
  33.3 0.9 broadcast_in_dim.14.bias
  34.2 0.0 copy-done.8
  34.2 0.3 broadcast.37.clone.1
  34.5 0.2 fusion.20
  34.7 1.8 pad_maximum_fusion.local
  36.5 0.0 copy-start.12
  36.5 25.2 %collective-permute-done.1 = bf16[640,1024]{1,0:T(8,128)(2,1)} collective-permute-done((bf16[640,1024]{1,0:T(8,128)(2,1)}, bf16[640,1024]{1,0:T(8,128)(2,1)}, u32[]{:S(2)}, u32[]{:S(2)}) %collective-permute-start.1) | collective-permute-done | bytes 1310752 | tf_op jit(solution)/shard_map/ppermute | solution.py:279
  61.7 1.5 constant_dynamic-update-slice_fusion.3
  63.2 0.0 copy-start.4
  63.2 0.0 copy-start.9
  63.2 2.6 %maximum_convert_fusion.1 = (bf16[640,512]{1,0:T(8,128)(2,1)S(1)}, f32[640,512]{1,0:T(8,128)}) fusion(bf16[640,2048]{1,0:T(8,128)(2,1)S(1)} %constant_dynamic-update-slice_fusion.3, bf16[2048,512]{1,0:T(8,128)(2,1)S(1)} %copy-done.12), kind=kOutput, calls=%fused_computation.38 | convolution fusion | flops 1342832640 | bytes 6684672 | tf_op jit(solution)/shard_map/dot_general | solution.py:254
  65.9 1.2 fusion.56
  67.1 5.8 %all-gather.3.cloned.1.call-done = bf16[17408,128]{1,0:T(8,128)(2,1)} async-done(((bf16[1088,128]{1,0:T(8,128)(2,1)}), bf16[17408,128]{1,0:T(8,128)(2,1)}) %all-gather.3.cloned.1.call-update) | async-done | bytes 4456464 | tf_op jit(solution)/shard_map/all_gather | solution.py:289
  72.8 0.0 copy-done.6
  72.9 1.0 slice.100
  73.8 4.1 %fusion.48 = (bf16[16,512,128]{2,1,0:T(8,128)(2,1)}, bf16[16,512,128]{2,1,0:T(8,128)(2,1)S(1)}) fusion(bf16[16,1088,128]{2,1,0:T(8,128)(2,1)} %bitcast.60), kind=kLoop, calls=%fused_computation.78 | loop fusion | bytes 8388608 | tf_op jit(solution)/shard_map/slice | solution.py:291
  77.9 1.4 fusion.51
  79.3 5.2 %multiply_reduce_fusion.1 = (f32[640]{0:T(1024)S(1)}, f32[640,256]{1,0:T(8,128)}) fusion(f32[640,256]{1,0:T(8,128)} %fusion.56, bf16[512,128]{1,0:T(8,128)(2,1)S(1)} %bitcast.70, bf16[512,128]{1,0:T(8,128)(2,1)S(1)} %bitcast.69, bf16[640,2048]{1,0:T(8,128)(2,1)} %copy-done.4, bf16[2048,128]{1,0:T(8,128)(2,1)} %bitcast.66, bf16[2048,128]{1,0:T(8,128)(2,1)} %bitcast.67, ...), kind=kOutput, calls=%fused_computation.45 | convolution fusion | flops 1520008576 | bytes 6294016 | tf_op jit(solution)/shard_map/dot_general | solution.py:254
  84.5 0.6 broadcast_multiply_fusion
  85.1 1.2 multiply_convert_fusion.normed
  86.3 2.0 fusion.65
  88.3 3.1 %fusion.50 = (bf16[16,1,256,128]{3,2,1,0:T(8,128)(2,1)}, bf16[16,1,256,128]{3,2,1,0:T(8,128)(2,1)}) fusion(bf16[16,2,256,128]{3,2,1,0:T(8,128)(2,1)} %bitcast.54), kind=kLoop, calls=%fused_computation.80 | loop fusion | bytes 4194304 | tf_op jit(solution)/shard_map/slice | solution.py:263
  91.4 1.2 copy.16.normed_t
  92.6 1.8 pad_maximum_fusion.1.queries
  94.4 0.0 copy-start.10
  94.4 42.9 %score.1 = (f32[16,256]{1,0:T(8,128)S(1)}, f32[640,256]{1,0:T(8,128)S(1)}, f32[4096,256]{1,0:T(8,128)}, bf16[1,1,640,1024]{3,2,1,0:T(8,128)(2,1)S(1)}) custom-call(bf16[2,640,1024]{2,1,0:T(8,128)(2,1)S(1)} %pad_maximum_fusion.local, bf16[4096,256]{1,0:T(8,128)(2,1)S(1)} %pad_maximum_fusion.1.queries, bf16[640,256]{1,0:T(8,128)(2,1)S(1)} %multiply_convert_fusion.normed, ...), custom_call_target="tpu_custom_call" | custom-call | tf_op jit(solution)/shard_map/score/pallas_call | solution.py:104
  137.3 0.0 copy-start.13
  137.3 0.2 multiply_reduce_fusion
  137.5 0.3 subtract_convert_fusion
  137.9 0.6 collective-permute-start.2
  138.5 1.2 bitcast_dynamic-update-slice_fusion
  139.7 4.8 %maximum_convert_fusion = (bf16[640,512]{1,0:T(8,128)(2,1)}, f32[640,512]{1,0:T(8,128)}) fusion(bf16[640,2048]{1,0:T(8,128)(2,1)} %bitcast_dynamic-update-slice_fusion, bf16[2048,512]{1,0:T(8,128)(2,1)S(1)} %copy-done.13), kind=kOutput, calls=%fused_computation.36 | convolution fusion | flops 1342832640 | bytes 6684672 | tf_op jit(solution)/shard_map/dot_general | solution.py:254
  144.5 2.5 %collective-permute-done.2 = bf16[640,256]{1,0:T(8,128)(2,1)S(1)} collective-permute-done((bf16[640,256]{1,0:T(8,128)(2,1)S(1)}, bf16[640,256]{1,0:T(8,128)(2,1)S(1)}, u32[]{:S(2)}, u32[]{:S(2)}) %collective-permute-start.2) | collective-permute-done | bytes 327712 | tf_op jit(solution)/shard_map/ppermute | solution.py:279
  147.0 0.7 copy-done.15
  147.7 8.0 %fusion = f32[2048,512]{1,0:T(8,128)} fusion(bf16[640,2048]{1,0:T(8,128)(2,1)} %bitcast_dynamic-update-slice_fusion, bf16[640,2048]{1,0:T(8,128)(2,1)S(1)} %copy-done.5, f32[640,512]{1,0:T(8,128)} %get-tuple-element.46, f32[640,512]{1,0:T(8,128)} %get-tuple-element.42, bf16[512,256]{1,0:T(8,128)(2,1)} %param.13, bf16[640,256]{1,0:T(8,128)(2,1)} %copy-done.15, ...), kind=kOutput, calls=%fused_computation.1 | convolution fusion | flops 3034316800 | bytes 12976128 | tf_op jit(solution)/shard_map/dot_general | solution.py:358
  155.7 4.1 %fusion.49 = (f32[1024,512]{1,0:T(8,128)}, f32[1024,512]{1,0:T(8,128)S(1)}) fusion(f32[2048,512]{1,0:T(8,128)} %fusion), kind=kLoop, calls=%fused_computation.79 | loop fusion | bytes 8388608 | tf_op jit(solution)/shard_map/slice | solution.py:373
  159.9 0.5 fusion.25
  160.4 61.2 %reduce_all.1 = (bf16[16,64,512]{2,1,0:T(8,128)(2,1)S(1)}, bf16[16,64,512]{2,1,0:T(8,128)(2,1)S(1)}, bf16[16,32,256]{2,1,0:T(8,128)(2,1)S(1)}, f32[1,128,256]{2,1,0:T(8,128)S(1)}) custom-call(f32[16,64,512]{2,1,0:T(8,128)S(1)} %bitcast.47, f32[16,64,512]{2,1,0:T(8,128)} %bitcast.53, f32[16,32,256]{2,1,0:T(8,128)S(1)} %bitcast.48, f32[32,128,256]{2,1,0:T(8,128)} %bitcast.61), custom_call_target="tpu_custom_call" | custom-call | tf_op jit(solution)/shard_map/reduce_all/pallas_call | solution.py:238
  221.6 0.7 fusion.37
  222.3 0.8 bitcast_convert_fusion.1
  223.2 0.2 pad_maximum_fusion.2
  223.4 2.7 %bitcast_convert_fusion = f32[2048,512]{1,0:T(8,128)} fusion(bf16[32,64,512]{2,1,0:T(8,128)(2,1)S(1)} %pad_maximum_fusion.2), kind=kLoop, calls=%fused_computation.22 | loop fusion | flops 1048576 | bytes 6291456 | tf_op jit(solution)/shard_map/convert_element_type | solution.py:378
  226.1 0.6 multiply_subtract_fusion
  (29 shorter events, 0.1 us)
Async XLA Ops:
  7.2 65.7 %all-gather.3.cloned.1.call-start = ((), (), s32[]{:S(2)}) async-start(), calls=%async_computation | async-start | bytes 4734976 | tf_op jit(solution)/shard_map/all_gather | solution.py:289
  11.7 6.8 %collective-permute-start = (bf16[576,128]{1,0:T(8,128)(2,1)S(1)}, bf16[576,128]{1,0:T(8,128)(2,1)S(1)}, u32[]{:S(2)}, u32[]{:S(2)}) collective-permute-start(bf16[576,128]{1,0:T(8,128)(2,1)S(1)} %constant_dynamic-update-slice_fusion), channel_id=1, source_target_pairs={{0,1},{1,0},{2,3},{3,2},{4,5},{5,4},{6,7},{7,6},{8,9},{9,8},{10,11... | collective-permute-start | bytes 442376 | tf_op jit(solution)/shard_map/ppermute | solution.py:279
  27.7 6.8 %copy-start.1 = (bf16[1024,1024]{1,0:T(8,128)(2,1)}, bf16[1024,1024]{1,0:T(8,128)(2,1)S(1)}, u32[]{:S(2)}) copy-start(bf16[1024,1024]{1,0:T(8,128)(2,1)S(1)} %gather_fusion) | copy-start | bytes 6291460
  27.7 1.9 copy-start.3
  29.6 3.6 %copy-start.14 = (bf16[1024]{0:T(1024)(128)(2,1)S(1)}, bf16[1024]{0:T(1024)(128)(2,1)}, u32[]{:S(2)}) copy-start(bf16[1024]{0:T(1024)(128)(2,1)} %param.11) | copy-start | bytes 6148
  29.6 4.6 %copy-start.8 = (bf16[256,256]{1,0:T(8,128)(2,1)S(1)}, bf16[256,256]{1,0:T(8,128)(2,1)}, u32[]{:S(2)}) copy-start(bf16[256,256]{1,0:T(8,128)(2,1)} %param.7) | copy-start | bytes 393220
  31.5 30.3 %collective-permute-start.1 = (bf16[640,1024]{1,0:T(8,128)(2,1)}, bf16[640,1024]{1,0:T(8,128)(2,1)}, u32[]{:S(2)}, u32[]{:S(2)}) collective-permute-start(bf16[640,1024]{1,0:T(8,128)(2,1)} %get-tuple-element.21), channel_id=1, source_target_pairs={{0,1},{1,0},{2,3},{3,2},{4,5},{5,4},{6,7},{7,6},{8,9},{9,8},{10,11... | collective-permute-start | bytes 3932168 | tf_op jit(solution)/shard_map/ppermute | solution.py:279
  36.5 26.7 %copy-start.12 = (bf16[2048,512]{1,0:T(8,128)(2,1)S(1)}, bf16[2048,512]{1,0:T(8,128)(2,1)}, u32[]{:S(2)}) copy-start(bf16[2048,512]{1,0:T(8,128)(2,1)} %param.12) | copy-start | bytes 6291460
  63.2 2.7 %copy-start.4 = (bf16[640,2048]{1,0:T(8,128)(2,1)}, bf16[640,2048]{1,0:T(8,128)(2,1)S(1)}, u32[]{:S(2)}) copy-start(bf16[640,2048]{1,0:T(8,128)(2,1)S(1)} %constant_dynamic-update-slice_fusion.3) | copy-start | bytes 7864324
  63.2 2.6 %copy-start.9 = (bf16[512,256]{1,0:T(8,128)(2,1)S(1)}, bf16[512,256]{1,0:T(8,128)(2,1)}, u32[]{:S(2)}) copy-start(bf16[512,256]{1,0:T(8,128)(2,1)} %param.13) | copy-start | bytes 786436
  65.9 7.0 %copy-start.6 = (bf16[640,512]{1,0:T(8,128)(2,1)}, bf16[640,512]{1,0:T(8,128)(2,1)S(1)}, u32[]{:S(2)}) copy-start(bf16[640,512]{1,0:T(8,128)(2,1)S(1)} %get-tuple-element.41) | copy-start | bytes 1966084
  92.6 1.8 copy-start
  94.4 42.9 %copy-start.2 = (f32[640,256]{1,0:T(8,128)S(1)}, f32[640,256]{1,0:T(8,128)}, u32[]{:S(2)}) copy-start(f32[640,256]{1,0:T(8,128)} %get-tuple-element.44) | copy-start | bytes 1966084
  94.4 43.1 %copy-start.10 = (f32[640]{0:T(1024)S(1)}, f32[640]{0:T(1024)}, u32[]{:S(2)}) copy-start(f32[640]{0:T(1024)} %get-tuple-element.38) | copy-start | bytes 7684
  94.4 43.1 %copy-start.11 = (f32[640]{0:T(1024)S(1)}, f32[640]{0:T(1024)}, u32[]{:S(2)}) copy-start(f32[640]{0:T(1024)} %get-tuple-element.39) | copy-start | bytes 7684
  137.3 2.4 %copy-start.13 = (bf16[2048,512]{1,0:T(8,128)(2,1)S(1)}, bf16[2048,512]{1,0:T(8,128)(2,1)}, u32[]{:S(2)}) copy-start(bf16[2048,512]{1,0:T(8,128)(2,1)} %param.12) | copy-start | bytes 6291460
  137.9 9.1 %collective-permute-start.2 = (bf16[640,256]{1,0:T(8,128)(2,1)S(1)}, bf16[640,256]{1,0:T(8,128)(2,1)S(1)}, u32[]{:S(2)}, u32[]{:S(2)}) collective-permute-start(bf16[640,256]{1,0:T(8,128)(2,1)S(1)} %subtract_convert_fusion), channel_id=1, source_target_pairs={{0,1},{1,0},{2,3},{3,2},{4,5},{5,4},{6,7},{7,6},{8,9},{9,8},{10,11... | collective-permute-start | bytes 983048 | tf_op jit(solution)/shard_map/ppermute | solution.py:279
  139.7 8.0 %copy-start.5 = (bf16[640,2048]{1,0:T(8,128)(2,1)S(1)}, bf16[640,2048]{1,0:T(8,128)(2,1)}, u32[]{:S(2)}) copy-start(bf16[640,2048]{1,0:T(8,128)(2,1)} %copy-done.4) | copy-start | bytes 7864324
  147.0 0.7 copy-start.15
  155.7 4.2 %copy-start.7 = (bf16[640,512]{1,0:T(8,128)(2,1)S(1)}, bf16[640,512]{1,0:T(8,128)(2,1)}, u32[]{:S(2)}) copy-start(bf16[640,512]{1,0:T(8,128)(2,1)} %copy-done.6) | copy-start | bytes 1966084
  155.7 4.2 %copy-start.16 = (bf16[640,256]{1,0:T(8,128)(2,1)S(1)}, bf16[640,256]{1,0:T(8,128)(2,1)}, u32[]{:S(2)}) copy-start(bf16[640,256]{1,0:T(8,128)(2,1)} %copy-done.15) | copy-start | bytes 983044
  155.7 4.2 %copy-start.17 = (bf16[640,512]{1,0:T(8,128)(2,1)S(1)}, bf16[640,512]{1,0:T(8,128)(2,1)}, u32[]{:S(2)}) copy-start(bf16[640,512]{1,0:T(8,128)(2,1)} %get-tuple-element.45) | copy-start | bytes 1966084
Sparse Core Ops, SparseCore 0:
  19.4 53.4 all-gather.2

commit v3 on v2

--- a/solution.py
+++ b/solution.py
@@ -9,10 +9,13 @@
 
 F32 = jnp.float32
 BF16 = jnp.bfloat16
-LANES = 128
 MESH = pl.DeviceIdType.MESH
 ANY = pl.BlockSpec(memory_space=pl.ANY)
 VMEM = pl.BlockSpec(memory_space=pltpu.VMEM)
+
+
+def mm(a, b):
+    return jnp.dot(a, b, preferred_element_type=F32)
 
 
 def bits_of(n):
@@ -49,7 +52,7 @@
         for t in range(1, groups):
             k = (s - 1) * (groups - 1) + t - 1
             copy = pltpu.make_async_remote_copy(
-                src_ref=local.at[lax.rem(member + s + t, groups)],
+                src_ref=local.at[(s + t) % groups],
                 dst_ref=rest_ref.at[s - 1, t - 1],
                 send_sem=fsend.at[k], recv_sem=frecv.at[k],
                 device_id={"group": others[s - 1]}, device_id_type=MESH)
@@ -126,23 +129,24 @@
     )(local, queries, normed, normed.T, bias)
 
 
-def reduce_kernel(plans, n_peers_of, *refs):
+def reduce_kernel(plans, n_in, n_peers_of, *refs):
     n = len(plans)
-    ins, outs = refs[:n], refs[n : 2 * n]
-    accs, sends, recvs = (refs[2 * n + i * n : 3 * n + i * n] for i in range(3))
-    send_sem, recv_sem, gsend, grecv = refs[5 * n :]
+    ins, refs = refs[:n_in], refs[n_in:]
+    outs = refs[:n]
+    accs, sends, recvs = (refs[n + i * n : 2 * n + i * n] for i in range(3))
+    send_sem, recv_sem, gsend, grecv = refs[4 * n :]
     greet([partner(a, b)[1] for a, b in n_peers_of])
     live = {}
 
     def begin(i, r):
-        rounds, bases, _ = plans[i]
+        rounds, bases, _, source, start, count = plans[i]
         bit, peer = partner(*rounds[r])
-        half = ins[i].shape[0] >> (r + 1)
-        at0 = ins[i].shape[0] - 2 * half
+        half = count >> (r + 1)
+        at0 = count - 2 * half
 
         def stage(j, carry):
             if r == 0:
-                block = ins[i][bases(j) + (1 - bit) * bases(half)]
+                block = ins[source][start + bases(j) + (1 - bit) * bases(half)]
             else:
                 block = accs[i][(1 - bit) * half + j]
             sends[i][at0 + j] = block.astype(BF16)
@@ -157,15 +161,15 @@
         live[i] = copy
 
     def finish(i, r):
-        rounds, bases, _ = plans[i]
+        rounds, bases, _, source, start, count = plans[i]
         bit, _ = partner(*rounds[r])
-        half = ins[i].shape[0] >> (r + 1)
-        at0 = ins[i].shape[0] - 2 * half
+        half = count >> (r + 1)
+        at0 = count - 2 * half
         live[i].wait()
 
         def add(j, carry):
             if r == 0:
-                block = ins[i][bases(j) + bit * bases(half)]
+                block = ins[source][start + bases(j) + bit * bases(half)]
             else:
                 block = accs[i][bit * half + j]
             accs[i][j] = block + recvs[i][at0 + j].astype(F32)
@@ -175,11 +179,11 @@
 
     def place(i, r):
         rounds = plans[i][0]
-        return sum(partner(*rounds[k])[0] * (ins[i].shape[0] >> (k + 1)) for k in range(r + 1))
+        return sum(partner(*rounds[k])[0] * (plans[i][5] >> (k + 1)) for k in range(r + 1))
 
     def share(i, r):
         peer = partner(*plans[i][0][r])[1]
-        span = pl.ds(place(i, r), ins[i].shape[0] >> (r + 1))
+        span = pl.ds(place(i, r), plans[i][5] >> (r + 1))
         copy = pltpu.make_async_remote_copy(
             src_ref=outs[i].at[span], dst_ref=outs[i].at[span],
             send_sem=gsend.at[i, r], recv_sem=grecv.at[i, r],
@@ -188,7 +192,7 @@
         live[i] = copy
 
     def advance(i, step):
-        rounds, _, gather = plans[i]
+        rounds, _, gather = plans[i][:3]
         k = len(rounds)
         if 0 < step <= k:
             finish(i, step - 1)
@@ -222,45 +226,32 @@
     return out
 
 
-def reduce_all(groups, n_dp, arrays):
+def reduce_all(groups, n_dp, xs, parts):
     plans = []
-    for x, rounds, gather in arrays:
-        n = x.shape[0]
+    for source, start, n, rounds, gather in parts:
         if gather:
             steps = [n >> (k + 1) for k in range(len(rounds))]
         else:
             steps = [b * groups if a == "dp" else b for a, b in rounds]
-        plans.append((rounds, functools.partial(bit_place, steps), gather))
-    xs = [x for x, _, _ in arrays]
+        bases = functools.partial(bit_place, steps)
+        plans.append((rounds, bases, gather, source, start, n))
+    shapes = [(p[5],) + xs[p[3]].shape[1:] for p in plans]
     most = max(len(p[0]) for p in plans)
     peers = [("dp", b) for b in bits_of(n_dp)] + [("group", b) for b in bits_of(groups)]
-    sems = pltpu.SemaphoreType.DMA((len(xs), most))
+    sems = pltpu.SemaphoreType.DMA((len(plans), most))
     return pl.pallas_call(
-        functools.partial(reduce_kernel, plans, peers),
+        functools.partial(reduce_kernel, plans, len(xs), peers),
         out_shape=tuple(
-            jax.ShapeDtypeStruct(x.shape, BF16) if g else jax.ShapeDtypeStruct((1,) + x.shape[1:], F32)
-            for x, _, g in arrays),
+            jax.ShapeDtypeStruct(shape, BF16) if p[2] else jax.ShapeDtypeStruct((1,) + shape[1:], F32)
+            for shape, p in zip(shapes, plans)),
         in_specs=[VMEM] * len(xs),
-        out_specs=(VMEM,) * len(xs),
-        scratch_shapes=[pltpu.VMEM((x.shape[0] // 2,) + x.shape[1:], F32) for x in xs]
-        + [pltpu.VMEM(x.shape, BF16) for x in xs] * 2 + [sems] * 4,
+        out_specs=(VMEM,) * len(plans),
+        scratch_shapes=[pltpu.VMEM((s[0] // 2,) + s[1:], F32) for s in shapes]
+        + [pltpu.VMEM(s, BF16) for s in shapes] * 2 + [sems] * 4,
         compiler_params=pltpu.CompilerParams(
             collective_id=1, has_side_effects=True, vmem_limit_bytes=48 << 20),
         name="reduce_all",
     )(*xs)
-
-
-def mm(a, b):
-    return jnp.dot(a, b, preferred_element_type=F32)
-
-
-def pack(x):
-    return jnp.concatenate([x[:, i : i + LANES] for i in range(0, x.shape[1], LANES)], 0)
-
-
-def unpack(x, rows, cols):
-    x = x.reshape(x.shape[0], cols // LANES, rows, LANES)
-    return jnp.concatenate([x[:, i].reshape(-1, LANES) for i in range(cols // LANES)], 1)
 
 
 def per_device(queries, item_features, corpus, sample_ids, sample_shift, w1, w2):
@@ -281,30 +272,61 @@
     def at(x, i):
         return lax.dynamic_index_in_dim(x, lax.rem(i, groups), 0, keepdims=False)
 
-    w1_rows, w2_rows = w1.shape[0] // n_dp, w2.shape[0] // n_dp
-    w1_piece = pack(lax.dynamic_slice_in_dim(w1, d * w1_rows, w1_rows))
-    w2_piece = pack(lax.dynamic_slice_in_dim(w2, d * w2_rows, w2_rows))
-    piece = jnp.concatenate([w1_piece, w2_piece], 0)
-    pieces = [pack(queries)] + [shift(piece, s) for s in range(1, groups)]
-    shared = lax.all_gather(jnp.concatenate(pieces, 0), "dp", axis=0, tiled=False)
-    nq, n1, n2 = pieces[0].shape[0], w1_piece.shape[0], w2_piece.shape[0]
-    q_all = unpack(shared[:, :nq], query_rows, emb)
+    def place_columns(parts):
+        if groups == 2:
+            swap = member == 0
+            return jnp.concatenate(
+                [jnp.where(swap, parts[0], parts[1]), jnp.where(swap, parts[1], parts[0])], 1)
+        out = jnp.zeros((parts[0].shape[0], groups * fg), BF16)
+        for s in range(groups):
+            start = lax.rem(member + groups - s, groups) * fg
+            out = lax.dynamic_update_slice_in_dim(out, parts[s], start, 1)
+        return out
+
+    q_all = lax.all_gather(queries, "dp", axis=0, tiled=True)
+
+    def swap_dp(x, step):
+        return lax.ppermute(x, "dp", [(i, i ^ step) for i in range(n_dp)])
+
+    quarter = lax.rem(d, 4)
+    odd, high = lax.rem(quarter, 2) == 1, quarter >= 2
+    w1_rows, w2_rows = w1.shape[0] // 4, w2.shape[0] // 4
+    piece = jnp.concatenate([
+        lax.dynamic_slice_in_dim(w1, quarter * w1_rows, w1_rows),
+        lax.dynamic_slice_in_dim(w2, quarter * w2_rows, w2_rows).reshape(-1, w1.shape[1]),
+    ], 0)
+    items = item_features.reshape(groups, quota, fg)
+    sample_ids, piece = lax.optimization_barrier((sample_ids, piece))
+    got = [shift(piece, s) for s in range(1, groups)]
+    ids = sample_ids.reshape(groups, negs)
+    item_parts = [shift(at(items, member + s), s) for s in range(1, groups)]
+    far_rows = [
+        corpus.at[at(ids, member + s)].get(mode="promise_in_bounds") for s in range(1, groups)
+    ]
+    picked_parts = [shift(far_rows[s - 1], s) for s in range(1, groups)]
+    own_ids, _ = lax.optimization_barrier((at(ids, member), far_rows))
+    own_rows = corpus.at[own_ids].get(mode="promise_in_bounds")
+    blocks = [jnp.concatenate([at(items, member), own_rows], 0)]
+    for s in range(1, groups):
+        blocks.append(jnp.concatenate([at(items, member + s), far_rows[s - 1]], 0))
+    local = jnp.stack(blocks[:1] if groups == 2 else blocks)
+
     w1s, w2s = [w1], [w2]
-    for s in range(1, groups):
-        at0 = nq + (s - 1) * (n1 + n2)
-        w1s.append(unpack(shared[:, at0 : at0 + n1], w1_rows, w1.shape[1]))
-        w2s.append(unpack(shared[:, at0 + n1 : at0 + n1 + n2], w2_rows, emb))
-
-    picked = corpus.at[sample_ids].get(mode="promise_in_bounds")
-    local = jnp.concatenate(
-        [item_features.reshape(groups, quota, fg), picked.reshape(groups, negs, fg)], 1
-    )
-    mine = [at(local, member)] + [shift(at(local, member + s), s) for s in range(1, groups)]
-    feats = jnp.zeros((rows, groups * fg), BF16)
-    for s in range(groups):
-        feats = lax.dynamic_update_slice_in_dim(
-            feats, mine[s], lax.rem(member + groups - s, groups) * fg, 1
-        )
+    for p0 in got:
+        p2 = swap_dp(p0, 2)
+        p1, p3 = swap_dp(p0, 1), swap_dp(p2, 1)
+        low = [jnp.where(odd, p1, p0), jnp.where(odd, p0, p1)]
+        upp = [jnp.where(odd, p3, p2), jnp.where(odd, p2, p3)]
+        placed = [jnp.where(high, u, l) for u, l in zip(upp, low)]
+        placed += [jnp.where(high, l, u) for u, l in zip(upp, low)]
+        w1s.append(jnp.concatenate([p[:w1_rows] for p in placed], 0))
+        w2s.append(jnp.concatenate([p[w1_rows:].reshape(-1, emb) for p in placed], 0))
+
+    feats = place_columns(
+        blocks[:1]
+        + [jnp.concatenate([a, b], 0) for a, b in zip(item_parts, picked_parts)]
+    )
+
     embedded = jnp.zeros((rows, emb), F32)
     pre_own = None
     for s in range(groups):
@@ -321,15 +343,9 @@
     log_total, grad_hat, query_part, landed = score(
         groups, n_dp, local, q_all, normed, bias[:, None])
     log_total = log_total.reshape(-1)
-    rest = jnp.zeros(((groups - 1) * rows, groups * fg), BF16)
-    for s in range(groups):
-        if s > 0:
-            blocks = landed[s - 1].reshape(-1, fg)
-        else:
-            blocks = jnp.concatenate([at(local, member + t) for t in range(1, groups)], 0)
-        rest = lax.dynamic_update_slice_in_dim(
-            rest, blocks, lax.rem(member + groups - s, groups) * fg, 1
-        )
+    rest = place_columns(
+        [jnp.concatenate(blocks[1:], 0)] + [landed[s - 1].reshape(-1, fg) for s in range(1, groups)]
+    )
 
     query_own = lax.dynamic_slice_in_dim(queries, member * quota, quota).astype(F32)
     positive_own = normed[:quota].astype(F32)
@@ -367,12 +383,16 @@
     )
     pad = -grad_w2.shape[0] % (16 * n_dp)
     padded = jnp.pad(grad_w2, ((0, pad), (0, 0)))
-    halves = grad_w1.reshape(2, n_dp, -1, grad_w1.shape[1])
-    out_a, out_b, out_w2, query_sum = reduce_all(groups, n_dp, [
-        (halves[0], along_last, True),
-        (halves[1], along_first, True),
-        (padded.reshape(n_dp, -1, emb), along_first, True),
-        (query_part.reshape(n_dp * groups, quota, emb), query_order, False),
+    xs = [
+        grad_w1.reshape(2 * n_dp, -1, grad_w1.shape[1]),
+        padded.reshape(n_dp, -1, emb),
+        query_part.reshape(n_dp * groups, quota, emb),
+    ]
+    out_a, out_b, out_w2, query_sum = reduce_all(groups, n_dp, xs, [
+        (0, 0, n_dp, along_last, True),
+        (0, n_dp, n_dp, along_first, True),
+        (1, 0, n_dp, along_first, True),
+        (2, 0, n_dp * groups, query_order, False),
     ])
     grad_query = scale * (query_sum[0] - positive_own)
     grad_w1 = jnp.concatenate([out_a, out_b], 0).reshape(grad_w1.shape).astype(F32)

time: 234 us -> 241 us (1.030)
  waiting for transfers between devices: 36.5 us -> 39.4 us
  starting transfers between devices: 5.35 us -> 7.77 us
    slice x7 -> x8, local copies, waits for them, and re-layouts: 14.6 us -> 5.81 us  [the longest x4 3.32 us: per_device(): w1s.append(jnp.concatenate([p[:w1_rows] for p in placed], 0))]
    ppermute x3 -> x4, waiting for transfers between devices: 30.7 us -> 37.3 us  [shift(): lax.ppermute(x, 'group', [(i, (i + s) % groups) for i in range(groups)])]
    reshape x0 -> x6, local copies, waits for them, and re-layouts: none -> 5.95 us  [the longest x4 5.91 us: per_device(): p[w1_rows:].reshape(-1, emb)]
    all_gather x1, waiting for transfers between devices: 5.78 us -> 0.01 us  [per_device(): q_all = lax.all_gather(queries, 'dp', axis=0, tiled=True)]
    gather x1 -> x2, local copies, waits for them, and re-layouts: 7.7 us -> 11.7 us  [the longest x1 6.2 us: per_device(): own_rows = corpus.at[own_ids].get(mode='promise_in_bounds')]
    concatenate x3 -> x1, other arithmetic: 4.39 us -> 0.85 us  [per_device(): jnp.concatenate([lax.dynamic_slice_in_dim(w1, quarter * w1_rows, w1_rows)...]
    select_n x0 -> x5, other arithmetic: none -> 3.14 us  [the longest x2 1.69 us: place_columns(): jnp.where(swap, parts[0], parts[1])]
    dynamic_update_slice x2 -> x0, local copies, waits for them, and re-layouts: 2.69 us -> none  [the longest x1 1.47 us: per_device(): lax.dynamic_update_slice_in_dim(feats, mine[s], lax.rem(member + groups -...]
  transfers between devices with their start and end apart: 4 -> 8, of which waited for: 4 -> 3; matrix products, arithmetic and copies ran while one was open for 12% -> 22% of each run, Pallas kernels for 0% -> 0%
where the time goes in v3:
time: 241 us; the launch traced here: 240 us
  Pallas kernels  106 us (44%)
  waiting for transfers between devices  39.4 us (16%)
  local copies, waits for them, and re-layouts  36.3 us (15%)
  matrix products  20.8 us (9%)
  other arithmetic  15.3 us (6%)
  between operations  14.3 us (6%)
  starting transfers between devices  7.77 us (3%)
    pallas_call x1, Pallas kernels, reduce_all(): pl.pallas_call(functools.partial(reduce_kernel, plans, len(xs), peers), o...  62 us
    pallas_call x1, Pallas kernels, score(): pl.pallas_call(functools.partial(score_kernel, groups, n_dp), out_shape=(...  43.8 us
    ppermute x4, waiting for transfers between devices, shift(): lax.ppermute(x, 'group', [(i, (i + s) % groups) for i in range(groups)])  37.3 us
    dot_general x4, matrix products, mm(): return jnp.dot(a, b, preferred_element_type=F32)  11.7 us
    dot_general x1, matrix products, per_device(): lax.dot_general(feats_all, grad_pre, over_rows, preferred_element_type=F32)  8.59 us
    unnamed x48, local copies, waits for them, and re-layouts  6.22 us
    gather x1, local copies, waits for them, and re-layouts, per_device(): own_rows = corpus.at[own_ids].get(mode='promise_in_bounds')  6.2 us
    reshape x4, local copies, waits for them, and re-layouts, per_device(): p[w1_rows:].reshape(-1, emb)  5.91 us
  transfers between devices with their start and end apart: 8, of which 3 were waited for; matrix products, arithmetic and copies ran while one was open for 22% of the time, Pallas kernels for 0%

profile of v3, /device:TPU:0, one launch (start us, length us, event | category | flops | bytes accessed | tf_op | source)
XLA Modules:
  0.0 239.6 jit_solution(2970636013838852720)
XLA Ops:
  7.2 0.0 copy-start
  7.2 0.0 all-gather.2.cloned.1.call-start
  7.2 0.7 all-gather.2.cloned.1.call-update
  7.9 0.8 constant_dynamic-slice_fusion.1
  8.9 0.9 pad_maximum_fusion.11
  9.8 0.0 copy-start.22
  9.8 5.5 %gather_fusion = bf16[512,1024]{1,0:T(8,128)(2,1)S(1)} fusion(bf16[2048,1024]{1,0:T(8,128)(2,1)} %param.9, s32[1024]{0:T(1024)S(1)} %pad_clamp_fusion.1), kind=kCustom, calls=%fused_computation | custom fusion | bytes 2099200 | tf_op jit(solution)/shard_map/gather | solution.py:304
  15.3 3.0 %collective-permute-start.1 = (bf16[512,1024]{1,0:T(8,128)(2,1)S(1)}, bf16[512,1024]{1,0:T(8,128)(2,1)}, u32[]{:S(2)}, u32[]{:S(2)}) collective-permute-start(bf16[512,1024]{1,0:T(8,128)(2,1)S(1)} %gather_fusion), channel_id=1, source_target_pairs={{0,1},{1,0},{2,3},{3,2},{4,5},{5,4},{6,7},{7,6},{8,9},{9,8},{10,11... | collective-permute-start | bytes 3145736 | tf_op jit(solution)/shard_map/ppermute | solution.py:270
  18.3 0.1 collective-permute-start.2
  18.4 1.8 dynamic-slice_bitcast_fusion.1
  20.1 1.9 collective-permute-start
  22.1 0.9 dynamic-slice_convert_fusion
  23.0 32.1 %collective-permute-done.2 = bf16[576,512]{1,0:T(8,128)(2,1)} collective-permute-done((bf16[576,512]{1,0:T(8,128)(2,1)}, bf16[576,512]{1,0:T(8,128)(2,1)}, u32[]{:S(2)}, u32[]{:S(2)}) %collective-permute-start.2) | collective-permute-done | bytes 589856 | tf_op jit(solution)/shard_map/ppermute | solution.py:270
  55.0 2.0 collective-permute-start.3
  57.1 0.1 convert_negate_fusion
  57.1 6.2 %gather_fusion.1 = bf16[512,1024]{1,0:T(8,128)(2,1)} fusion(bf16[2048,1024]{1,0:T(8,128)(2,1)} %param.9, s32[1024]{0:T(1024)S(1)} %pad_clamp_fusion), kind=kCustom, calls=%fused_computation.1 | custom fusion | bytes 2099200 | tf_op jit(solution)/shard_map/gather | solution.py:308
  63.3 0.9 broadcast_in_dim.7.bias
  64.2 1.1 constant_dynamic-update-slice_fusion.1
  65.3 0.1 collective-permute-start.5
  65.4 1.3 constant_dynamic-update-slice_fusion
  66.7 1.0 broadcast_select_fusion.1
  67.7 1.3 collective-permute-done.3
  69.0 2.6 %maximum_convert_fusion.2 = (bf16[640,512]{1,0:T(8,128)(2,1)S(1)}, f32[640,512]{1,0:T(8,128)}) fusion(bf16[2048,512]{1,0:T(8,128)(2,1)S(1)} %copy-done, bf16[640,1024]{1,0:T(8,128)(2,1)S(1)} %get-tuple-element.29, bf16[640,1024]{1,0:T(8,128)(2,1)S(1)} %get-tuple-element.28), kind=kOutput, calls=%fused_computation.39 | convolution fusion | flops 1348075520 | bytes 6684672 | tf_op jit(solution)/shard_map/dot_general | solution.py:18
  71.7 1.2 fusion.53
  72.9 1.4 broadcast_select_fusion.9
  74.3 0.8 slice.40
  75.2 0.6 slice.44
  75.8 0.8 slice.41
  76.6 0.6 slice.45
  77.2 0.8 slice.42
  78.1 0.6 slice.46
  78.7 0.8 slice.43
  79.5 0.6 slice.47
  80.1 1.5 reshape.93
  81.6 1.5 reshape.94
  83.1 1.5 reshape.95
  84.6 1.5 reshape.96
  86.0 5.2 %multiply_reduce_fusion.1 = (f32[640]{0:T(1024)S(1)}, f32[640,256]{1,0:T(8,128)}) fusion(f32[640,256]{1,0:T(8,128)} %fusion.53, bf16[128,256]{1,0:T(8,128)(2,1)} %reshape.96, bf16[128,256]{1,0:T(8,128)(2,1)} %reshape.95, bf16[128,256]{1,0:T(8,128)(2,1)} %reshape.94, bf16[128,256]{1,0:T(8,128)(2,1)} %reshape.93, bf16[512,512]{1,0:T(8,128)(2,1)} %slice.43, ...), kind=kOutput, calls=%fused_computation.48 | convolution fusion | flops 1525775744 | bytes 6294016 | tf_op jit(solution)/shard_map/dot_general | solution.py:18
  91.3 2.0 fusion.59
  93.3 1.9 copy.16.normed_t
  95.1 2.0 multiply_convert_fusion.normed
  97.1 1.6 copy-done.1
  98.7 1.0 copy-done.2
  99.7 1.0 copy-done.3
  100.7 1.0 copy-done.4
  101.6 43.8 %score.1 = (f32[16,256]{1,0:T(8,128)S(1)}, f32[640,256]{1,0:T(8,128)S(1)}, f32[4096,256]{1,0:T(8,128)}, bf16[1,1,640,1024]{3,2,1,0:T(8,128)(2,1)S(1)}) custom-call(bf16[1,640,1024]{2,1,0:T(8,128)(2,1)S(1)} %get-tuple-element.34.local, bf16[4096,256]{1,0:T(8,128)(2,1)S(1)} %copy-done.1, bf16[640,256]{1,0:T(8,128)(2,1)S(1)} %copy-done.2, ...), custom_call_target="tpu_custom_call" | custom-call | tf_op jit(solution)/shard_map/score/pallas_call | solution.py:107
  145.4 0.2 multiply_reduce_fusion
  145.6 0.3 subtract_convert_fusion
  145.9 0.6 collective-permute-start.6
  146.5 0.1 copy-done.7
  146.6 0.0 copy-done.14
  146.6 0.7 bitcast_select_fusion.1
  147.4 2.6 %maximum_convert_fusion = (bf16[640,512]{1,0:T(8,128)(2,1)S(1)}, f32[640,512]{1,0:T(8,128)}) fusion(bf16[2048,512]{1,0:T(8,128)(2,1)S(1)} %copy-done, bf16[640,1024]{1,0:T(8,128)(2,1)S(1)} %get-tuple-element.27, bf16[640,1024]{1,0:T(8,128)(2,1)S(1)} %get-tuple-element.26), kind=kOutput, calls=%fused_computation.37 | convolution fusion | flops 1348075520 | bytes 6684672 | tf_op jit(solution)/shard_map/dot_general | solution.py:18
  150.0 5.3 %collective-permute-done.6 = bf16[640,256]{1,0:T(8,128)(2,1)S(1)} collective-permute-done((bf16[640,256]{1,0:T(8,128)(2,1)S(1)}, bf16[640,256]{1,0:T(8,128)(2,1)S(1)}, u32[]{:S(2)}, u32[]{:S(2)}) %collective-permute-start.6) | collective-permute-done | bytes 327712 | tf_op jit(solution)/shard_map/ppermute | solution.py:270
  155.3 0.5 fusion.22
  155.9 0.4 copy-done.20
  156.3 8.6 %fusion = f32[2048,512]{1,0:T(8,128)} fusion(bf16[640,1024]{1,0:T(8,128)(2,1)} %copy-done.12, bf16[640,1024]{1,0:T(8,128)(2,1)} %copy-done.11, bf16[640,1024]{1,0:T(8,128)(2,1)} %copy-done.10, bf16[640,1024]{1,0:T(8,128)(2,1)} %copy-done.9, bf16[512,256]{1,0:T(8,128)(2,1)S(1)} %copy-done.20, f32[640,512]{1,0:T(8,128)} %get-tuple-element.47, ...), kind=kOutput, calls=%fused_computation.2 | convolution fusion | flops 3044802560 | bytes 12976128 | tf_op jit(solution)/shard_map/dot_general | solution.py:374
  164.9 62.0 %reduce_all.1 = (bf16[16,64,512]{2,1,0:T(8,128)(2,1)S(1)}, bf16[16,64,512]{2,1,0:T(8,128)(2,1)S(1)}, bf16[16,32,256]{2,1,0:T(8,128)(2,1)S(1)}, f32[1,128,256]{2,1,0:T(8,128)S(1)}) custom-call(f32[32,64,512]{2,1,0:T(8,128)} %bitcast.37, f32[16,32,256]{2,1,0:T(8,128)S(1)} %bitcast.34, f32[32,128,256]{2,1,0:T(8,128)} %bitcast.36), custom_call_target="tpu_custom_call" | custom-call | tf_op jit(solution)/shard_map/reduce_all/pallas_call | solution.py:242
  226.9 0.2 pad_maximum_fusion.1
  227.1 0.0 copy-start.18
  227.1 2.7 %bitcast_convert_fusion = f32[2048,512]{1,0:T(8,128)} fusion(bf16[32,64,512]{2,1,0:T(8,128)(2,1)S(1)} %pad_maximum_fusion.1), kind=kLoop, calls=%fused_computation.27 | loop fusion | flops 1048576 | bytes 6291456 | tf_op jit(solution)/shard_map/convert_element_type | solution.py:398
  229.8 0.8 bitcast_convert_fusion.1
  230.7 1.5 fusion.40
  232.2 0.6 multiply_subtract_fusion
  (53 shorter events, 0.2 us)
Async XLA Ops:
  7.2 1.7 copy-start
  7.2 2.6 %copy-start.21 = (s32[1024]{0:T(1024)S(1)}, s32[1024]{0:T(1024)}, u32[]{:S(2)}) copy-start(s32[1024]{0:T(1024)} %param.10) | copy-start | bytes 12292
  7.2 89.9 %all-gather.2.cloned.1.call-start = ((), (), s32[]{:S(2)}) async-start(), calls=%async_computation | async-start | bytes 2228224 | tf_op jit(solution)/shard_map/all_gather | solution.py:286
  9.8 47.3 %copy-start.22 = (bf16[1024]{0:T(1024)(128)(2,1)S(1)}, bf16[1024]{0:T(1024)(128)(2,1)}, u32[]{:S(2)}) copy-start(bf16[1024]{0:T(1024)(128)(2,1)} %param.11) | copy-start | bytes 6148
  15.3 48.1 %copy-start.6 = (bf16[512,1024]{1,0:T(8,128)(2,1)}, bf16[512,1024]{1,0:T(8,128)(2,1)S(1)}, u32[]{:S(2)}) copy-start(bf16[512,1024]{1,0:T(8,128)(2,1)S(1)} %gather_fusion) | copy-start | bytes 3145732
  15.3 50.1 %collective-permute-start.1 = (bf16[512,1024]{1,0:T(8,128)(2,1)S(1)}, bf16[512,1024]{1,0:T(8,128)(2,1)}, u32[]{:S(2)}, u32[]{:S(2)}) collective-permute-start(bf16[512,1024]{1,0:T(8,128)(2,1)S(1)} %gather_fusion), channel_id=1, source_target_pairs={{0,1},{1,0},{2,3},{3,2},{4,5},{5,4},{6,7},{7,6},{8,9},{9,8},{10,11... | collective-permute-start | bytes 3145736 | tf_op jit(solution)/shard_map/ppermute | solution.py:270
  18.3 36.7 %collective-permute-start.2 = (bf16[576,512]{1,0:T(8,128)(2,1)}, bf16[576,512]{1,0:T(8,128)(2,1)}, u32[]{:S(2)}, u32[]{:S(2)}) collective-permute-start(bf16[576,512]{1,0:T(8,128)(2,1)} %pad_maximum_fusion.11), channel_id=1, source_target_pairs={{0,1},{1,0},{2,3},{3,2},{4,5},{5,4},{6,7},{7,6},{8,9},{9,8},{10,11... | collective-permute-start | bytes 1769480 | tf_op jit(solution)/shard_map/ppermute | solution.py:270
  20.1 43.2 %copy-start.13 = (bf16[128,1024]{1,0:T(8,128)(2,1)}, bf16[128,1024]{1,0:T(8,128)(2,1)S(1)}, u32[]{:S(2)}) copy-start(bf16[128,1024]{1,0:T(8,128)(2,1)S(1)} %get-tuple-element.36) | copy-start | bytes 786436
  20.1 44.1 %collective-permute-start = (bf16[128,1024]{1,0:T(8,128)(2,1)S(1)}, bf16[128,1024]{1,0:T(8,128)(2,1)}, u32[]{:S(2)}, u32[]{:S(2)}) collective-permute-start(bf16[128,1024]{1,0:T(8,128)(2,1)S(1)} %get-tuple-element.36), channel_id=1, source_target_pairs={{0,1},{1,0},{2,3},{3,2},{4,5},{5,4},{6,7},{7,6},{8,9},{9,8},{10,11... | collective-permute-start | bytes 786440 | tf_op jit(solution)/shard_map/ppermute | solution.py:270
  55.0 14.0 %collective-permute-start.3 = (bf16[576,512]{1,0:T(8,128)(2,1)}, bf16[576,512]{1,0:T(8,128)(2,1)}, u32[]{:S(2)}, u32[]{:S(2)}) collective-permute-start(bf16[576,512]{1,0:T(8,128)(2,1)} %collective-permute-done.2), channel_id=1, source_target_pairs={{0,4},{2,6},{4,0},{6,2},{8,12},{10,14},{12,8},{14,10},{16,20},{18,... | collective-permute-start | bytes 1769480 | tf_op jit(solution)/shard_map/ppermute | solution.py:289
  64.2 2.5 %copy-start.8 = (bf16[512,1024]{1,0:T(8,128)(2,1)S(1)}, bf16[512,1024]{1,0:T(8,128)(2,1)}, u32[]{:S(2)}) copy-start(bf16[512,1024]{1,0:T(8,128)(2,1)} %gather_fusion.1) | copy-start | bytes 3145732
  64.2 2.5 %copy-start.15 = (bf16[128,1024]{1,0:T(8,128)(2,1)S(1)}, bf16[128,1024]{1,0:T(8,128)(2,1)}, u32[]{:S(2)}) copy-start(bf16[128,1024]{1,0:T(8,128)(2,1)} %get-tuple-element.35) | copy-start | bytes 786436
  65.3 7.6 %collective-permute-start.5 = (bf16[576,512]{1,0:T(8,128)(2,1)}, bf16[576,512]{1,0:T(8,128)(2,1)S(1)}, u32[]{:S(2)}, u32[]{:S(2)}) collective-permute-start(bf16[576,512]{1,0:T(8,128)(2,1)} %collective-permute-done.2), channel_id=1, source_target_pairs={{0,2},{2,0},{4,6},{6,4},{8,10},{10,8},{12,14},{14,12},{16,18},{18,... | collective-permute-start | bytes 1769480 | tf_op jit(solution)/shard_map/ppermute | solution.py:289
  67.7 4.0 %copy-start.9 = (bf16[640,1024]{1,0:T(8,128)(2,1)}, bf16[640,1024]{1,0:T(8,128)(2,1)S(1)}, u32[]{:S(2)}) copy-start(bf16[640,1024]{1,0:T(8,128)(2,1)S(1)} %get-tuple-element.28) | copy-start | bytes 3932164
  67.7 4.0 %copy-start.10 = (bf16[640,1024]{1,0:T(8,128)(2,1)}, bf16[640,1024]{1,0:T(8,128)(2,1)S(1)}, u32[]{:S(2)}) copy-start(bf16[640,1024]{1,0:T(8,128)(2,1)S(1)} %get-tuple-element.29) | copy-start | bytes 3932164
  69.0 3.8 %collective-permute-start.4 = (bf16[576,512]{1,0:T(8,128)(2,1)}, bf16[576,512]{1,0:T(8,128)(2,1)S(1)}, u32[]{:S(2)}, u32[]{:S(2)}) collective-permute-start(bf16[576,512]{1,0:T(8,128)(2,1)} %collective-permute-done.3), channel_id=1, source_target_pairs={{0,2},{2,0},{4,6},{6,4},{8,10},{10,8},{12,14},{14,12},{16,18},{18,... | collective-permute-start | bytes 1769480 | tf_op jit(solution)/shard_map/ppermute | solution.py:289
  69.0 2.7 %copy-start.19 = (bf16[512,256]{1,0:T(8,128)(2,1)S(1)}, bf16[512,256]{1,0:T(8,128)(2,1)}, u32[]{:S(2)}) copy-start(bf16[512,256]{1,0:T(8,128)(2,1)} %param.13) | copy-start | bytes 786436
  71.7 1.2 copy-start.16
  97.1 1.6 copy-start.1
  98.7 1.0 copy-start.2
  99.7 1.0 copy-start.3
  100.6 1.0 copy-start.4
  101.6 43.8 %copy-start.5 = (f32[640,256]{1,0:T(8,128)S(1)}, f32[640,256]{1,0:T(8,128)}, u32[]{:S(2)}) copy-start(f32[640,256]{1,0:T(8,128)} %get-tuple-element.45) | copy-start | bytes 1966084
  145.4 1.2 copy-start.7
  145.4 1.3 copy-start.14
  145.9 9.4 %collective-permute-start.6 = (bf16[640,256]{1,0:T(8,128)(2,1)S(1)}, bf16[640,256]{1,0:T(8,128)(2,1)S(1)}, u32[]{:S(2)}, u32[]{:S(2)}) collective-permute-start(bf16[640,256]{1,0:T(8,128)(2,1)S(1)} %subtract_convert_fusion), channel_id=1, source_target_pairs={{0,1},{1,0},{2,3},{3,2},{4,5},{5,4},{6,7},{7,6},{8,9},{9,8},{10,11... | collective-permute-start | bytes 983048 | tf_op jit(solution)/shard_map/ppermute | solution.py:270
  147.4 2.7 %copy-start.11 = (bf16[640,1024]{1,0:T(8,128)(2,1)}, bf16[640,1024]{1,0:T(8,128)(2,1)S(1)}, u32[]{:S(2)}) copy-start(bf16[640,1024]{1,0:T(8,128)(2,1)S(1)} %get-tuple-element.26) | copy-start | bytes 3932164
  147.4 2.6 %copy-start.12 = (bf16[640,1024]{1,0:T(8,128)(2,1)}, bf16[640,1024]{1,0:T(8,128)(2,1)S(1)}, u32[]{:S(2)}) copy-start(bf16[640,1024]{1,0:T(8,128)(2,1)S(1)} %get-tuple-element.27) | copy-start | bytes 3932164
  147.4 7.9 %copy-start.17 = (bf16[640,512]{1,0:T(8,128)(2,1)S(1)}, bf16[640,512]{1,0:T(8,128)(2,1)}, u32[]{:S(2)}) copy-start(bf16[640,512]{1,0:T(8,128)(2,1)} %copy-done.16) | copy-start | bytes 1966084
  155.3 1.0 copy-start.20
  227.1 3.6 %copy-start.18 = (bf16[256,256]{1,0:T(8,128)(2,1)S(1)}, bf16[256,256]{1,0:T(8,128)(2,1)}, u32[]{:S(2)}) copy-start(bf16[256,256]{1,0:T(8,128)(2,1)} %param.7) | copy-start | bytes 393220
Sparse Core Ops, SparseCore 0:
  10.2 43.9 all-gather.1

commit v4 on v3

--- a/solution.py
+++ b/solution.py
@@ -35,9 +35,9 @@
     pl.semaphore_wait(barrier, len(peers))
 
 
-def score_kernel(groups, n_dp, local, queries, normed, normed_t, bias,
+def score_kernel(groups, n_dp, local, queries_in, normed, normed_t, bias,
                  total_ref, hat_ref, part_ref, rest_ref,
-                 logits, stats, arrived, send_sem, recv_sem, fsend, frecv):
+                 queries, logits, stats, arrived, qsem, send_sem, recv_sem, fsend, frecv):
     tiles, cols, width = logits.shape
     emb = normed.shape[1]
     scale = emb ** (-0.5)
@@ -46,6 +46,8 @@
     peers = [partner(a, b)[1] for a, b in rounds]
     others = [lax.rem(member + s, groups) for s in range(1, groups)]
     extra = [{"group": o} for o in others] if groups > 2 else []
+    fetch = pltpu.make_async_copy(queries_in, queries, qsem)
+    fetch.start()
     greet(peers + extra)
     copies = []
     for s in range(1, groups):
@@ -69,6 +71,7 @@
         stats[0, 1, pl.ds(i, 1), :] = jnp.sum(jnp.exp(block - top), 0, keepdims=True)
         return carry
 
+    fetch.wait()
     lax.fori_loop(0, tiles, first, 0)
     for r, peer in enumerate(peers):
         copy = pltpu.make_async_remote_copy(
@@ -112,12 +115,14 @@
             jax.ShapeDtypeStruct((total, emb), F32),
             jax.ShapeDtypeStruct((groups - 1, groups - 1, rows, fg), BF16),
         ),
-        in_specs=[ANY, VMEM, VMEM, VMEM, VMEM],
+        in_specs=[ANY, ANY, VMEM, VMEM, VMEM],
         out_specs=(VMEM, VMEM, VMEM, ANY),
         scratch_shapes=[
+            pltpu.VMEM((total, emb), BF16),
             pltpu.VMEM((tiles, rows, width), F32),
             pltpu.VMEM((rounds + 1, 2, tiles, width), F32),
             pltpu.VMEM((rounds, 2, tiles, width), F32),
+            pltpu.SemaphoreType.DMA,
             pltpu.SemaphoreType.DMA((rounds,)),
             pltpu.SemaphoreType.DMA((rounds,)),
             pltpu.SemaphoreType.DMA((n_copies,)),
@@ -288,24 +293,34 @@
     def swap_dp(x, step):
         return lax.ppermute(x, "dp", [(i, i ^ step) for i in range(n_dp)])
 
+    def beside(x, cols):
+        if x.shape[1] <= cols:
+            return jnp.concatenate(jnp.split(x, cols // x.shape[1], 0), 1)
+        return jnp.concatenate(jnp.split(x, x.shape[1] // cols, 1), 0)
+
+    def restored(x, cols):
+        if cols <= x.shape[1]:
+            return jnp.concatenate(jnp.split(x, x.shape[1] // cols, 1), 0)
+        return jnp.concatenate(jnp.split(x, cols // x.shape[1], 0), 1)
+
     quarter = lax.rem(d, 4)
     odd, high = lax.rem(quarter, 2) == 1, quarter >= 2
     w1_rows, w2_rows = w1.shape[0] // 4, w2.shape[0] // 4
     piece = jnp.concatenate([
         lax.dynamic_slice_in_dim(w1, quarter * w1_rows, w1_rows),
-        lax.dynamic_slice_in_dim(w2, quarter * w2_rows, w2_rows).reshape(-1, w1.shape[1]),
+        beside(lax.dynamic_slice_in_dim(w2, quarter * w2_rows, w2_rows), w1.shape[1]),
     ], 0)
     items = item_features.reshape(groups, quota, fg)
     sample_ids, piece = lax.optimization_barrier((sample_ids, piece))
     got = [shift(piece, s) for s in range(1, groups)]
     ids = sample_ids.reshape(groups, negs)
-    item_parts = [shift(at(items, member + s), s) for s in range(1, groups)]
     far_rows = [
         corpus.at[at(ids, member + s)].get(mode="promise_in_bounds") for s in range(1, groups)
     ]
+    far_rows, items, got = lax.optimization_barrier((far_rows, items, got))
+    item_parts = [shift(at(items, member + s), s) for s in range(1, groups)]
     picked_parts = [shift(far_rows[s - 1], s) for s in range(1, groups)]
-    own_ids, _ = lax.optimization_barrier((at(ids, member), far_rows))
-    own_rows = corpus.at[own_ids].get(mode="promise_in_bounds")
+    own_rows = corpus.at[at(ids, member)].get(mode="promise_in_bounds")
     blocks = [jnp.concatenate([at(items, member), own_rows], 0)]
     for s in range(1, groups):
         blocks.append(jnp.concatenate([at(items, member + s), far_rows[s - 1]], 0))
@@ -320,7 +335,7 @@
         placed = [jnp.where(high, u, l) for u, l in zip(upp, low)]
         placed += [jnp.where(high, l, u) for u, l in zip(upp, low)]
         w1s.append(jnp.concatenate([p[:w1_rows] for p in placed], 0))
-        w2s.append(jnp.concatenate([p[w1_rows:].reshape(-1, emb) for p in placed], 0))
+        w2s.append(jnp.concatenate([restored(p[w1_rows:], emb) for p in placed], 0))
 
     feats = place_columns(
         blocks[:1]

time: 241 us -> 228 us (0.946)
  waiting for transfers between devices: 39.4 us -> 29.7 us
  local copies, waits for them, and re-layouts: 36.3 us -> 33.4 us
    ppermute x4, waiting for transfers between devices: 37.3 us -> 29.7 us  [shift(): lax.ppermute(x, 'group', [(i, (i + s) % groups) for i in range(groups)])]
    reshape x5 -> x0, local copies, waits for them, and re-layouts: 5.94 us -> none  [the longest x4 5.91 us: per_device(): p[w1_rows:].reshape(-1, emb)]
    unnamed x48 -> x55, local copies, waits for them, and re-layouts: 6.22 us -> 11 us
    slice x4 -> x0, local copies, waits for them, and re-layouts: 2.49 us -> none  [per_device(): p[w1_rows:].reshape(-1, emb)]
  transfers between devices with their start and end apart: 8 -> 8, of which waited for: 3 -> 3; matrix products, arithmetic and copies ran while one was open for 22% -> 20% of each run, Pallas kernels for 0% -> 0%
where the time goes in v4:
time: 228 us; the launch traced here: 227 us
  Pallas kernels  106 us (46%)
  local copies, waits for them, and re-layouts  33.4 us (15%)
  waiting for transfers between devices  29.7 us (13%)
  matrix products  20.8 us (9%)
  other arithmetic  15.4 us (7%)
  between operations  14.3 us (6%)
  starting transfers between devices  7.46 us (3%)
    pallas_call x1, Pallas kernels, reduce_all(): pl.pallas_call(functools.partial(reduce_kernel, plans, len(xs), peers), o...  62.1 us
    pallas_call x1, Pallas kernels, score(): pl.pallas_call(functools.partial(score_kernel, groups, n_dp), out_shape=(...  44 us
    ppermute x4, waiting for transfers between devices, shift(): lax.ppermute(x, 'group', [(i, (i + s) % groups) for i in range(groups)])  29.7 us
    dot_general x4, matrix products, mm(): return jnp.dot(a, b, preferred_element_type=F32)  11.7 us
    unnamed x55, local copies, waits for them, and re-layouts  11 us
    dot_general x1, matrix products, per_device(): lax.dot_general(feats_all, grad_pre, over_rows, preferred_element_type=F32)  8.59 us
    gather x1, local copies, waits for them, and re-layouts, per_device(): own_rows = corpus.at[at(ids, member)].get(mode='promise_in_bounds')  6.21 us
    ppermute x4, starting transfers between devices, shift(): lax.ppermute(x, 'group', [(i, (i + s) % groups) for i in range(groups)])  5.79 us
  transfers between devices with their start and end apart: 8, of which 3 were waited for; matrix products, arithmetic and copies ran while one was open for 20% of the time, Pallas kernels for 0%

profile of v4, /device:TPU:0, one launch (start us, length us, event | category | flops | bytes accessed | tf_op | source)
XLA Modules:
  0.0 227.1 jit_solution(15367139911487402381)
XLA Ops:
  7.2 0.0 copy-start
  7.2 0.0 all-gather.2.cloned.1.call-start
  7.3 0.9 constant_dynamic-slice_fusion
  8.2 0.6 copy-done
  8.8 0.9 maximum_maximum_fusion
  9.7 3.0 %collective-permute-start = (bf16[576,512]{1,0:T(8,128)(2,1)}, bf16[576,512]{1,0:T(8,128)(2,1)}, u32[]{:S(2)}, u32[]{:S(2)}) collective-permute-start(bf16[576,512]{1,0:T(8,128)(2,1)} %maximum_maximum_fusion), channel_id=1, source_target_pairs={{0,1},{1,0},{2,3},{3,2},{4,5},{5,4},{6,7},{7,6},{8,9},{9,8},{10,11... | collective-permute-start | bytes 1769480 | tf_op jit(solution)/shard_map/ppermute | solution.py:275
  12.7 5.5 %gather_fusion = bf16[512,1024]{1,0:T(8,128)(2,1)S(1)} fusion(bf16[2048,1024]{1,0:T(8,128)(2,1)} %param.9, s32[1024]{0:T(1024)S(1)} %pad_clamp_fusion.1), kind=kCustom, calls=%fused_computation | custom fusion | bytes 2099200 | tf_op jit(solution)/shard_map/gather | solution.py:318
  18.2 8.1 %collective-permute-done = bf16[576,512]{1,0:T(8,128)(2,1)} collective-permute-done((bf16[576,512]{1,0:T(8,128)(2,1)}, bf16[576,512]{1,0:T(8,128)(2,1)}, u32[]{:S(2)}, u32[]{:S(2)}) %collective-permute-start) | collective-permute-done | bytes 589856 | tf_op jit(solution)/shard_map/ppermute | solution.py:275
  26.3 1.7 collective-permute-start.2
  28.0 1.5 collective-permute-start.3
  29.5 0.0 all-gather.2.cloned.1.call-update
  29.6 1.8 dynamic-slice_bitcast_fusion.1
  31.3 0.5 collective-permute-start.1
  31.8 6.2 %gather_fusion.1 = bf16[512,1024]{1,0:T(8,128)(2,1)} fusion(bf16[2048,1024]{1,0:T(8,128)(2,1)} %param.9, s32[1024]{0:T(1024)S(1)} %pad_clamp_fusion), kind=kCustom, calls=%fused_computation.1 | custom fusion | bytes 2099200 | tf_op jit(solution)/shard_map/gather | solution.py:323
  38.1 0.1 convert_negate_fusion
  38.2 0.9 broadcast_in_dim.4.bias
  39.0 1.0 dynamic-slice_convert_fusion
  40.0 0.1 collective-permute-start.5
  40.1 16.3 %collective-permute-done.1 = bf16[128,1024]{1,0:T(8,128)(2,1)} collective-permute-done((bf16[128,1024]{1,0:T(8,128)(2,1)S(1)}, bf16[128,1024]{1,0:T(8,128)(2,1)}, u32[]{:S(2)}, u32[]{:S(2)}) %collective-permute-start.1) | collective-permute-done | bytes 262176 | tf_op jit(solution)/shard_map/ppermute | solution.py:275
  56.4 1.0 constant_dynamic-update-slice_fusion.1
  57.3 0.1 collective-permute-start.4
  57.4 1.3 constant_dynamic-update-slice_fusion
  58.8 1.0 broadcast_select_fusion.1
  59.8 2.6 %maximum_convert_fusion.2 = (bf16[640,512]{1,0:T(8,128)(2,1)S(1)}, f32[640,512]{1,0:T(8,128)}) fusion(bf16[2048,512]{1,0:T(8,128)(2,1)S(1)} %copy-done, bf16[640,1024]{1,0:T(8,128)(2,1)S(1)} %get-tuple-element.33, bf16[640,1024]{1,0:T(8,128)(2,1)S(1)} %get-tuple-element.32), kind=kOutput, calls=%fused_computation.39 | convolution fusion | flops 1348075520 | bytes 6684672 | tf_op jit(solution)/shard_map/dot_general | solution.py:18
  62.4 1.2 fusion.46
  63.6 1.4 broadcast_select_fusion.6
  65.0 0.8 slice.36
  65.9 0.8 slice.37
  66.7 0.8 slice.38
  67.5 0.8 slice.39
  68.4 0.6 slice_dynamic-update-slice_fusion.7
  69.0 0.6 slice_dynamic-update-slice_fusion.6
  69.6 0.6 slice_dynamic-update-slice_fusion.5
  70.2 0.6 slice_dynamic-update-slice_fusion.4
  70.8 0.6 slice_dynamic-update-slice_fusion.3
  71.4 0.6 slice_dynamic-update-slice_fusion.2
  72.0 0.6 slice_dynamic-update-slice_fusion.1
  72.6 0.6 slice_dynamic-update-slice_fusion
  73.2 5.2 %multiply_reduce_fusion.1 = (f32[640]{0:T(1024)S(1)}, f32[640,256]{1,0:T(8,128)}) fusion(f32[640,256]{1,0:T(8,128)} %fusion.46, bf16[512,256]{1,0:T(8,128)(2,1)} %slice_dynamic-update-slice_fusion, bf16[512,512]{1,0:T(8,128)(2,1)} %slice.39, bf16[512,512]{1,0:T(8,128)(2,1)} %slice.38, bf16[512,512]{1,0:T(8,128)(2,1)} %slice.37, ...), kind=kOutput, calls=%fused_computation.48 | convolution fusion | flops 1524727168 | bytes 6294016 | tf_op jit(solution)/shard_map/dot_general | solution.py:18
  78.5 2.0 fusion.53
  80.4 1.9 copy.16.normed_t
  82.3 2.0 multiply_convert_fusion.normed
  84.3 1.6 copy-done.1
  85.9 1.0 copy-done.2
  86.8 1.0 copy-done.3
  87.8 1.0 copy-done.4
  88.8 44.0 %score.1 = (f32[16,256]{1,0:T(8,128)S(1)}, f32[640,256]{1,0:T(8,128)S(1)}, f32[4096,256]{1,0:T(8,128)}, bf16[1,1,640,1024]{3,2,1,0:T(8,128)(2,1)S(1)}) custom-call(bf16[1,640,1024]{2,1,0:T(8,128)(2,1)S(1)} %get-tuple-element.38.local, bf16[4096,256]{1,0:T(8,128)(2,1)S(1)} %copy-done.1, bf16[640,256]{1,0:T(8,128)(2,1)S(1)} %copy-done.2, ...), custom_call_target="tpu_custom_call" | custom-call | tf_op jit(solution)/shard_map/score/pallas_call | solution.py:110
  132.8 0.2 multiply_reduce_fusion
  133.0 0.3 subtract_convert_fusion
  133.4 0.6 collective-permute-start.6
  133.9 0.1 copy-done.7
  134.0 0.0 copy-done.14
  134.1 0.7 bitcast_select_fusion.1
  134.9 2.6 %maximum_convert_fusion = (bf16[640,512]{1,0:T(8,128)(2,1)S(1)}, f32[640,512]{1,0:T(8,128)}) fusion(bf16[2048,512]{1,0:T(8,128)(2,1)S(1)} %copy-done, bf16[640,1024]{1,0:T(8,128)(2,1)S(1)} %get-tuple-element.31, bf16[640,1024]{1,0:T(8,128)(2,1)S(1)} %get-tuple-element.30), kind=kOutput, calls=%fused_computation.37 | convolution fusion | flops 1348075520 | bytes 6684672 | tf_op jit(solution)/shard_map/dot_general | solution.py:18
  137.5 5.3 %collective-permute-done.6 = bf16[640,256]{1,0:T(8,128)(2,1)S(1)} collective-permute-done((bf16[640,256]{1,0:T(8,128)(2,1)S(1)}, bf16[640,256]{1,0:T(8,128)(2,1)S(1)}, u32[]{:S(2)}, u32[]{:S(2)}) %collective-permute-start.6) | collective-permute-done | bytes 327712 | tf_op jit(solution)/shard_map/ppermute | solution.py:275
  142.8 0.5 fusion.22
  143.3 0.4 copy-done.20
  143.7 8.6 %fusion = f32[2048,512]{1,0:T(8,128)} fusion(bf16[640,1024]{1,0:T(8,128)(2,1)} %copy-done.12, bf16[640,1024]{1,0:T(8,128)(2,1)} %copy-done.11, bf16[640,1024]{1,0:T(8,128)(2,1)} %copy-done.10, bf16[640,1024]{1,0:T(8,128)(2,1)} %copy-done.9, bf16[512,256]{1,0:T(8,128)(2,1)S(1)} %copy-done.20, f32[640,512]{1,0:T(8,128)} %get-tuple-element.55, ...), kind=kOutput, calls=%fused_computation.2 | convolution fusion | flops 3044802560 | bytes 12976128 | tf_op jit(solution)/shard_map/dot_general | solution.py:389
  152.3 62.1 %reduce_all.1 = (bf16[16,64,512]{2,1,0:T(8,128)(2,1)S(1)}, bf16[16,64,512]{2,1,0:T(8,128)(2,1)S(1)}, bf16[16,32,256]{2,1,0:T(8,128)(2,1)S(1)}, f32[1,128,256]{2,1,0:T(8,128)S(1)}) custom-call(f32[32,64,512]{2,1,0:T(8,128)} %bitcast.40, f32[16,32,256]{2,1,0:T(8,128)S(1)} %bitcast.37, f32[32,128,256]{2,1,0:T(8,128)} %bitcast.39), custom_call_target="tpu_custom_call" | custom-call | tf_op jit(solution)/shard_map/reduce_all/pallas_call | solution.py:247
  214.4 0.2 pad_maximum_fusion.1
  214.6 2.7 %bitcast_convert_fusion = f32[2048,512]{1,0:T(8,128)} fusion(bf16[32,64,512]{2,1,0:T(8,128)(2,1)S(1)} %pad_maximum_fusion.1), kind=kLoop, calls=%fused_computation.27 | loop fusion | flops 1048576 | bytes 6291456 | tf_op jit(solution)/shard_map/convert_element_type | solution.py:413
  217.3 0.8 bitcast_convert_fusion.1
  218.2 1.5 fusion.33
  219.7 0.6 multiply_subtract_fusion
  (50 shorter events, 0.2 us)
Async XLA Ops:
  7.2 1.6 copy-start
  7.2 5.5 %copy-start.21 = (s32[1024]{0:T(1024)S(1)}, s32[1024]{0:T(1024)}, u32[]{:S(2)}) copy-start(s32[1024]{0:T(1024)} %param.10) | copy-start | bytes 12292
  7.2 77.1 %all-gather.2.cloned.1.call-start = ((), (), s32[]{:S(2)}) async-start(), calls=%async_computation | async-start | bytes 2228224 | tf_op jit(solution)/shard_map/all_gather | solution.py:291
  9.7 16.6 %collective-permute-start = (bf16[576,512]{1,0:T(8,128)(2,1)}, bf16[576,512]{1,0:T(8,128)(2,1)}, u32[]{:S(2)}, u32[]{:S(2)}) collective-permute-start(bf16[576,512]{1,0:T(8,128)(2,1)} %maximum_maximum_fusion), channel_id=1, source_target_pairs={{0,1},{1,0},{2,3},{3,2},{4,5},{5,4},{6,7},{7,6},{8,9},{9,8},{10,11... | collective-permute-start | bytes 1769480 | tf_op jit(solution)/shard_map/ppermute | solution.py:275
  18.2 19.9 %copy-start.6 = (bf16[512,1024]{1,0:T(8,128)(2,1)}, bf16[512,1024]{1,0:T(8,128)(2,1)S(1)}, u32[]{:S(2)}) copy-start(bf16[512,1024]{1,0:T(8,128)(2,1)S(1)} %gather_fusion) | copy-start | bytes 3145732
  26.3 31.1 %collective-permute-start.2 = (bf16[512,1024]{1,0:T(8,128)(2,1)S(1)}, bf16[512,1024]{1,0:T(8,128)(2,1)}, u32[]{:S(2)}, u32[]{:S(2)}) collective-permute-start(bf16[512,1024]{1,0:T(8,128)(2,1)S(1)} %gather_fusion), channel_id=1, source_target_pairs={{0,1},{1,0},{2,3},{3,2},{4,5},{5,4},{6,7},{7,6},{8,9},{9,8},{10,11... | collective-permute-start | bytes 3145736 | tf_op jit(solution)/shard_map/ppermute | solution.py:275
  28.0 29.3 %collective-permute-start.3 = (bf16[576,512]{1,0:T(8,128)(2,1)}, bf16[576,512]{1,0:T(8,128)(2,1)}, u32[]{:S(2)}, u32[]{:S(2)}) collective-permute-start(bf16[576,512]{1,0:T(8,128)(2,1)} %collective-permute-done), channel_id=1, source_target_pairs={{0,4},{2,6},{4,0},{6,2},{8,12},{10,14},{12,8},{14,10},{16,20},{18,... | collective-permute-start | bytes 1769480 | tf_op jit(solution)/shard_map/ppermute | solution.py:294
  31.3 6.7 %copy-start.13 = (bf16[128,1024]{1,0:T(8,128)(2,1)}, bf16[128,1024]{1,0:T(8,128)(2,1)S(1)}, u32[]{:S(2)}) copy-start(bf16[128,1024]{1,0:T(8,128)(2,1)S(1)} %get-tuple-element.40) | copy-start | bytes 786436
  31.3 25.0 %collective-permute-start.1 = (bf16[128,1024]{1,0:T(8,128)(2,1)S(1)}, bf16[128,1024]{1,0:T(8,128)(2,1)}, u32[]{:S(2)}, u32[]{:S(2)}) collective-permute-start(bf16[128,1024]{1,0:T(8,128)(2,1)S(1)} %get-tuple-element.40), channel_id=1, source_target_pairs={{0,1},{1,0},{2,3},{3,2},{4,5},{5,4},{6,7},{7,6},{8,9},{9,8},{10,11... | collective-permute-start | bytes 786440 | tf_op jit(solution)/shard_map/ppermute | solution.py:275
  31.8 6.2 %copy-start.22 = (bf16[1024]{0:T(1024)(128)(2,1)S(1)}, bf16[1024]{0:T(1024)(128)(2,1)}, u32[]{:S(2)}) copy-start(bf16[1024]{0:T(1024)(128)(2,1)} %param.11) | copy-start | bytes 6148
  39.0 19.7 %copy-start.8 = (bf16[512,1024]{1,0:T(8,128)(2,1)S(1)}, bf16[512,1024]{1,0:T(8,128)(2,1)}, u32[]{:S(2)}) copy-start(bf16[512,1024]{1,0:T(8,128)(2,1)} %gather_fusion.1) | copy-start | bytes 3145732
  39.0 19.7 %copy-start.15 = (bf16[128,1024]{1,0:T(8,128)(2,1)S(1)}, bf16[128,1024]{1,0:T(8,128)(2,1)}, u32[]{:S(2)}) copy-start(bf16[128,1024]{1,0:T(8,128)(2,1)} %get-tuple-element.39) | copy-start | bytes 786436
  40.0 23.6 %collective-permute-start.5 = (bf16[576,512]{1,0:T(8,128)(2,1)}, bf16[576,512]{1,0:T(8,128)(2,1)S(1)}, u32[]{:S(2)}, u32[]{:S(2)}) collective-permute-start(bf16[576,512]{1,0:T(8,128)(2,1)} %collective-permute-done), channel_id=1, source_target_pairs={{0,2},{2,0},{4,6},{6,4},{8,10},{10,8},{12,14},{14,12},{16,18},{18,... | collective-permute-start | bytes 1769480 | tf_op jit(solution)/shard_map/ppermute | solution.py:294
  57.3 6.2 %collective-permute-start.4 = (bf16[576,512]{1,0:T(8,128)(2,1)}, bf16[576,512]{1,0:T(8,128)(2,1)S(1)}, u32[]{:S(2)}, u32[]{:S(2)}) collective-permute-start(bf16[576,512]{1,0:T(8,128)(2,1)} %collective-permute-done.3), channel_id=1, source_target_pairs={{0,2},{2,0},{4,6},{6,4},{8,10},{10,8},{12,14},{14,12},{16,18},{18,... | collective-permute-start | bytes 1769480 | tf_op jit(solution)/shard_map/ppermute | solution.py:294
  59.7 2.7 %copy-start.9 = (bf16[640,1024]{1,0:T(8,128)(2,1)}, bf16[640,1024]{1,0:T(8,128)(2,1)S(1)}, u32[]{:S(2)}) copy-start(bf16[640,1024]{1,0:T(8,128)(2,1)S(1)} %get-tuple-element.32) | copy-start | bytes 3932164
  59.7 2.7 %copy-start.10 = (bf16[640,1024]{1,0:T(8,128)(2,1)}, bf16[640,1024]{1,0:T(8,128)(2,1)S(1)}, u32[]{:S(2)}) copy-start(bf16[640,1024]{1,0:T(8,128)(2,1)S(1)} %get-tuple-element.33) | copy-start | bytes 3932164
  59.7 2.7 %copy-start.19 = (bf16[512,256]{1,0:T(8,128)(2,1)S(1)}, bf16[512,256]{1,0:T(8,128)(2,1)}, u32[]{:S(2)}) copy-start(bf16[512,256]{1,0:T(8,128)(2,1)} %param.13) | copy-start | bytes 786436
  62.4 1.2 copy-start.16
  84.3 1.6 copy-start.1
  85.9 1.0 copy-start.2
  86.8 1.0 copy-start.3
  87.8 1.0 copy-start.4
  88.8 44.1 %copy-start.5 = (f32[640,256]{1,0:T(8,128)S(1)}, f32[640,256]{1,0:T(8,128)}, u32[]{:S(2)}) copy-start(f32[640,256]{1,0:T(8,128)} %get-tuple-element.53) | copy-start | bytes 1966084
  132.8 1.2 copy-start.7
  132.8 1.3 copy-start.14
  133.4 9.4 %collective-permute-start.6 = (bf16[640,256]{1,0:T(8,128)(2,1)S(1)}, bf16[640,256]{1,0:T(8,128)(2,1)S(1)}, u32[]{:S(2)}, u32[]{:S(2)}) collective-permute-start(bf16[640,256]{1,0:T(8,128)(2,1)S(1)} %subtract_convert_fusion), channel_id=1, source_target_pairs={{0,1},{1,0},{2,3},{3,2},{4,5},{5,4},{6,7},{7,6},{8,9},{9,8},{10,11... | collective-permute-start | bytes 983048 | tf_op jit(solution)/shard_map/ppermute | solution.py:275
  134.8 2.7 %copy-start.11 = (bf16[640,1024]{1,0:T(8,128)(2,1)}, bf16[640,1024]{1,0:T(8,128)(2,1)S(1)}, u32[]{:S(2)}) copy-start(bf16[640,1024]{1,0:T(8,128)(2,1)S(1)} %get-tuple-element.30) | copy-start | bytes 3932164
  134.8 2.7 %copy-start.12 = (bf16[640,1024]{1,0:T(8,128)(2,1)}, bf16[640,1024]{1,0:T(8,128)(2,1)S(1)}, u32[]{:S(2)}) copy-start(bf16[640,1024]{1,0:T(8,128)(2,1)S(1)} %get-tuple-element.31) | copy-start | bytes 3932164
  134.9 7.9 %copy-start.17 = (bf16[640,512]{1,0:T(8,128)(2,1)S(1)}, bf16[640,512]{1,0:T(8,128)(2,1)}, u32[]{:S(2)}) copy-start(bf16[640,512]{1,0:T(8,128)(2,1)} %copy-done.16) | copy-start | bytes 1966084
  142.8 1.0 copy-start.20
  214.6 3.6 %copy-start.18 = (bf16[256,256]{1,0:T(8,128)(2,1)S(1)}, bf16[256,256]{1,0:T(8,128)(2,1)}, u32[]{:S(2)}) copy-start(bf16[256,256]{1,0:T(8,128)(2,1)} %param.7) | copy-start | bytes 393220
Sparse Core Ops, SparseCore 0:
  29.7 41.4 all-gather.1
